TPU v7x, 512 devices: a whole 4x8x8 slice. The times are simulated.
512 devices in a mesh: row: 32 (over y, x), col: 16 (over z, core).
Axes of the slice: x: 4, y: 8, z: 8, core: 2. Of those that a mesh axis runs over, the one named last changes fastest.
Arguments:
- points: float32 [8, 65536], P(None, ('row', 'col')), may hold values from -1.8 to 1.8
- inverse_scale: float32 [8], replicated, may hold values from 0.5 to 1
- targets: float32 [16, 65536], P(None, ('row', 'col')), may hold values from -3.5 to 5.5
- noise_var: float32 [16], replicated, may hold values from 0.5 to 2
Outputs:
- solution: float32 [16, 65536], P(None, ('row', 'col'))
- residual: float32 [16, 65536], P(None, ('row', 'col'))
All inputs are finite; a program needn't handle non-finite values.
Results may differ from a plain program's by a relative error of at most 0.0015.
Values sent between devices are 32-bit elements; how exact they have to be, the bound alone decides.
No kernel may reach another device: no remote copies, remote signals or barrier semaphores. Data moves between devices by JAX's collectives and lax.ppermute only.
A program may use at most 64 MiB of HBM per device.

v0:
```python
import jax
import jax.numpy as jnp
from jax import lax
from jax.sharding import PartitionSpec as P

ITERS = 2


exact_mode = lax.Precision.HIGHEST


def block_terms(row_z, row_half, col_z, col_v):
    col_half = 0.5 * jnp.sum(col_z * col_z, axis=0)
    inner_products = jnp.einsum("fb,fr->br", col_z, row_z, precision=exact_mode)
    kernel = jnp.exp(inner_products - col_half[:, None] - row_half[None, :])
    return jnp.dot(col_v, kernel, precision=exact_mode, preferred_element_type=jnp.float32)


def slab_width(row_count):
    block_cols = max(128, 1048576 // row_count)
    return block_cols


def kernel_terms(row_z, row_half, col_z, col_v):
    column_count = col_z.shape[1]
    block_cols = slab_width(row_z.shape[1])
    block_count = column_count // block_cols
    z_slabs = col_z.reshape(col_z.shape[0], block_count, block_cols).transpose(1, 0, 2)
    v_slabs = col_v.reshape(col_v.shape[0], block_count, block_cols).transpose(1, 0, 2)

    def advance(accumulated, slabs):
        return (accumulated + block_terms(row_z, row_half, slabs[0], slabs[1]), None)

    initial = jnp.zeros((col_v.shape[0], row_z.shape[1]), jnp.float32)
    accumulated, unused = lax.scan(advance, initial, (z_slabs, v_slabs))
    return accumulated


def squares(residual):
    return lax.psum(jnp.sum(residual * residual, axis=1), ("row", "col"))


def on_device(points, inverse_scale, targets, noise_var):
    scaled = points * inverse_scale[:, None]
    all_scaled = lax.all_gather(scaled, ("row", "col"), axis=1, tiled=True)
    row_half = 0.5 * jnp.sum(scaled * scaled, axis=0)
    solution = jnp.zeros_like(targets)
    residual = targets
    direction = targets
    norm_now = squares(residual)
    for turn in range(ITERS):
        image = (
            kernel_terms(
                scaled,
                row_half,
                all_scaled,
                lax.all_gather(direction, ("row", "col"), axis=1, tiled=True),
            )
            + noise_var[:, None] * direction
        )
        curvature = lax.psum(jnp.sum(direction * image, axis=1), ("row", "col"))
        step_size = norm_now / curvature
        solution = solution + step_size[:, None] * direction
        residual = residual - step_size[:, None] * image
        norm_next = squares(residual)
        direction = residual + (norm_next / norm_now)[:, None] * direction
        norm_now = norm_next
    return (solution, residual)


def solution(mesh):
    return jax.shard_map(
        on_device,
        mesh=mesh,
        in_specs=(P(None, ("row", "col")), P(), P(None, ("row", "col")), P()),
        out_specs=(P(None, ("row", "col")), P(None, ("row", "col"))),
        check_vma=False,
    )
```

profile of v0, /device:TPU:1, one launch (start us, length us, event | category | flops | bytes accessed | tf_op | source)
XLA Modules:
  0.0 937.4 jit_solution(9115898685250048283)
XLA Ops:
  9.4 127.9 %all-gather.4.cloned.1.call-done = f32[16,65536]{1,0:T(8,128)} async-done(((f32[16,128]{1,0:T(8,128)}), f32[16,65536]{1,0:T(8,128)}) %all-gather.4.cloned.1.call-update) | async-done | bytes 4194320 | tf_op jit(solution)/shard_map/all_gather | solution.py:57
  143.8 110.4 %all-gather.6.cloned.1.call-done = f32[8,65536]{1,0:T(8,128)} async-done(((f32[8,128]{1,0:T(8,128)}), f32[8,65536]{1,0:T(8,128)}) %all-gather.6.cloned.1.call-update) | async-done | bytes 2097168 | tf_op jit(solution)/shard_map/all_gather | solution.py:45
  254.3 143.0 %while.22 = (s32[]{:T(128)}, f32[16,128]{1,0:T(8,128)S(1)}, f32[8,16,8192]{2,0,1:T(8,128)}, f32[8,8,8192]{2,1,0:T(8,128)}, f32[8,128]{1,0:T(8,128)S(1)}, /*index=5*/f32[128]{0:T(128)S(1)}, s32[]{:T(128)}, s32[]{:T(128)}) while((s32[]{:T(128)}, f32[16,128]{1,0:T(8,128)S(1)}, f32[8,16,8192]{2,0,1:T(8,128)}, f32[8,8,8192]{2,1,0:T(8,128)}, ...), condition=%wide.region_5.6_spmd.clone, body=%wide.region_3.5_spmd.clone.sunk | while | flops 304222208 | bytes 10638439 | solution.py:35
  255.3 10.0 %fusion.34 = f32[8192,128]{1,0:T(8,128)} fusion(f32[8,128]{1,0:T(8,128)S(1)} %get-tuple-element.242, f32[128]{0:T(128)S(1)} %get-tuple-element.243, f32[8192]{0:T(1024)S(1)} %broadcast_multiply_fusion.7, f32[8,8,8192]{2,1,0:T(8,128)} %get-tuple-element.241, s32[]{:T(128)} %get-tuple-element.230), kind=kOutput, calls=%fused_computation.2.clone.1 | convolution fusion | flops 102760448 | bytes 4494336 | tf_op jit(solution)/shard_map/while/body/eval_jaxpr/fb,fr->br/dot_general | solution.py:14
  273.2 10.0 %fusion.34 = f32[8192,128]{1,0:T(8,128)} fusion(f32[8,128]{1,0:T(8,128)S(1)} %get-tuple-element.242, f32[128]{0:T(128)S(1)} %get-tuple-element.243, f32[8192]{0:T(1024)S(1)} %broadcast_multiply_fusion.7, f32[8,8,8192]{2,1,0:T(8,128)} %get-tuple-element.241, s32[]{:T(128)} %get-tuple-element.230), kind=kOutput, calls=%fused_computation.2.clone.1 | convolution fusion | flops 102760448 | bytes 4494336 | tf_op jit(solution)/shard_map/while/body/eval_jaxpr/fb,fr->br/dot_general | solution.py:14
  291.1 10.0 %fusion.34 = f32[8192,128]{1,0:T(8,128)} fusion(f32[8,128]{1,0:T(8,128)S(1)} %get-tuple-element.242, f32[128]{0:T(128)S(1)} %get-tuple-element.243, f32[8192]{0:T(1024)S(1)} %broadcast_multiply_fusion.7, f32[8,8,8192]{2,1,0:T(8,128)} %get-tuple-element.241, s32[]{:T(128)} %get-tuple-element.230), kind=kOutput, calls=%fused_computation.2.clone.1 | convolution fusion | flops 102760448 | bytes 4494336 | tf_op jit(solution)/shard_map/while/body/eval_jaxpr/fb,fr->br/dot_general | solution.py:14
  308.9 10.0 %fusion.34 = f32[8192,128]{1,0:T(8,128)} fusion(f32[8,128]{1,0:T(8,128)S(1)} %get-tuple-element.242, f32[128]{0:T(128)S(1)} %get-tuple-element.243, f32[8192]{0:T(1024)S(1)} %broadcast_multiply_fusion.7, f32[8,8,8192]{2,1,0:T(8,128)} %get-tuple-element.241, s32[]{:T(128)} %get-tuple-element.230), kind=kOutput, calls=%fused_computation.2.clone.1 | convolution fusion | flops 102760448 | bytes 4494336 | tf_op jit(solution)/shard_map/while/body/eval_jaxpr/fb,fr->br/dot_general | solution.py:14
  326.8 10.0 %fusion.34 = f32[8192,128]{1,0:T(8,128)} fusion(f32[8,128]{1,0:T(8,128)S(1)} %get-tuple-element.242, f32[128]{0:T(128)S(1)} %get-tuple-element.243, f32[8192]{0:T(1024)S(1)} %broadcast_multiply_fusion.7, f32[8,8,8192]{2,1,0:T(8,128)} %get-tuple-element.241, s32[]{:T(128)} %get-tuple-element.230), kind=kOutput, calls=%fused_computation.2.clone.1 | convolution fusion | flops 102760448 | bytes 4494336 | tf_op jit(solution)/shard_map/while/body/eval_jaxpr/fb,fr->br/dot_general | solution.py:14
  344.7 10.0 %fusion.34 = f32[8192,128]{1,0:T(8,128)} fusion(f32[8,128]{1,0:T(8,128)S(1)} %get-tuple-element.242, f32[128]{0:T(128)S(1)} %get-tuple-element.243, f32[8192]{0:T(1024)S(1)} %broadcast_multiply_fusion.7, f32[8,8,8192]{2,1,0:T(8,128)} %get-tuple-element.241, s32[]{:T(128)} %get-tuple-element.230), kind=kOutput, calls=%fused_computation.2.clone.1 | convolution fusion | flops 102760448 | bytes 4494336 | tf_op jit(solution)/shard_map/while/body/eval_jaxpr/fb,fr->br/dot_general | solution.py:14
  362.6 10.0 %fusion.34 = f32[8192,128]{1,0:T(8,128)} fusion(f32[8,128]{1,0:T(8,128)S(1)} %get-tuple-element.242, f32[128]{0:T(128)S(1)} %get-tuple-element.243, f32[8192]{0:T(1024)S(1)} %broadcast_multiply_fusion.7, f32[8,8,8192]{2,1,0:T(8,128)} %get-tuple-element.241, s32[]{:T(128)} %get-tuple-element.230), kind=kOutput, calls=%fused_computation.2.clone.1 | convolution fusion | flops 102760448 | bytes 4494336 | tf_op jit(solution)/shard_map/while/body/eval_jaxpr/fb,fr->br/dot_general | solution.py:14
  380.4 10.0 %fusion.34 = f32[8192,128]{1,0:T(8,128)} fusion(f32[8,128]{1,0:T(8,128)S(1)} %get-tuple-element.242, f32[128]{0:T(128)S(1)} %get-tuple-element.243, f32[8192]{0:T(1024)S(1)} %broadcast_multiply_fusion.7, f32[8,8,8192]{2,1,0:T(8,128)} %get-tuple-element.241, s32[]{:T(128)} %get-tuple-element.230), kind=kOutput, calls=%fused_computation.2.clone.1 | convolution fusion | flops 102760448 | bytes 4494336 | tf_op jit(solution)/shard_map/while/body/eval_jaxpr/fb,fr->br/dot_general | solution.py:14
  397.4 96.5 %all-reduce = (f32[16]{0:T(128)S(1)}, f32[16]{0:T(128)S(1)}) all-reduce(f32[16]{0:T(128)S(1)} %get-tuple-element.117, f32[16]{0:T(128)S(1)} %get-tuple-element.116), channel_id=1, replica_groups=mesh['row'=32,'col'=16] {'row','col'}, use_global_device_ids=true, to_apply=%region_1.0 | all-reduce | flops 32 | bytes 256 | tf_op jit(solution)/shard_map/psum | solution.py:40
  494.1 93.8 %psum.30 = f32[16]{0:T(128)S(1)} all-reduce(f32[16]{0:T(128)S(1)} %multiply_reduce_fusion.1), channel_id=1, replica_groups=mesh['row'=32,'col'=16] {'row','col'}, use_global_device_ids=true, to_apply=%region_9.10 | all-reduce | flops 16 | bytes 128 | tf_op jit(solution)/shard_map/psum | solution.py:40
  588.6 115.1 %all-gather.8.cloned.1.call-done = f32[16,65536]{1,0:T(8,128)} async-done(((f32[16,128]{1,0:T(8,128)}), f32[16,65536]{1,0:T(8,128)}) %all-gather.8.cloned.1.call-update) | async-done | bytes 4194320 | tf_op jit(solution)/shard_map/all_gather | solution.py:57
  708.2 125.0 %while.23 = (s32[]{:T(128)}, f32[16,128]{1,0:T(8,128)S(1)}, f32[8,16,8192]{2,1,0:T(8,128)}, f32[8,8,8192]{2,1,0:T(8,128)}, f32[8,128]{1,0:T(8,128)S(1)}, /*index=5*/f32[128]{0:T(128)S(1)}, s32[]{:T(128)}, s32[]{:T(128)}) while((s32[]{:T(128)}, f32[16,128]{1,0:T(8,128)S(1)}, f32[8,16,8192]{2,1,0:T(8,128)}, ...), condition=%wide.region_12.13_spmd.clone, body=%wide.region_10.12_spmd.clone.sunk | while | flops 304222208 | bytes 9590371 | solution.py:35
  709.3 10.0 %fusion.40 = f32[8192,128]{1,0:T(8,128)} fusion(f32[8,128]{1,0:T(8,128)S(1)} %get-tuple-element.266, f32[128]{0:T(128)S(1)} %get-tuple-element.267, f32[8192]{0:T(1024)S(1)} %broadcast_multiply_fusion.8, f32[8,8,8192]{2,1,0:T(8,128)} %get-tuple-element.265, s32[]{:T(128)} %get-tuple-element.254), kind=kOutput, calls=%fused_computation.14.clone.1 | convolution fusion | flops 102760448 | bytes 4494336 | tf_op jit(solution)/shard_map/while/body/eval_jaxpr/fb,fr->br/dot_general | solution.py:14
  724.9 10.0 %fusion.40 = f32[8192,128]{1,0:T(8,128)} fusion(f32[8,128]{1,0:T(8,128)S(1)} %get-tuple-element.266, f32[128]{0:T(128)S(1)} %get-tuple-element.267, f32[8192]{0:T(1024)S(1)} %broadcast_multiply_fusion.8, f32[8,8,8192]{2,1,0:T(8,128)} %get-tuple-element.265, s32[]{:T(128)} %get-tuple-element.254), kind=kOutput, calls=%fused_computation.14.clone.1 | convolution fusion | flops 102760448 | bytes 4494336 | tf_op jit(solution)/shard_map/while/body/eval_jaxpr/fb,fr->br/dot_general | solution.py:14
  740.5 10.0 %fusion.40 = f32[8192,128]{1,0:T(8,128)} fusion(f32[8,128]{1,0:T(8,128)S(1)} %get-tuple-element.266, f32[128]{0:T(128)S(1)} %get-tuple-element.267, f32[8192]{0:T(1024)S(1)} %broadcast_multiply_fusion.8, f32[8,8,8192]{2,1,0:T(8,128)} %get-tuple-element.265, s32[]{:T(128)} %get-tuple-element.254), kind=kOutput, calls=%fused_computation.14.clone.1 | convolution fusion | flops 102760448 | bytes 4494336 | tf_op jit(solution)/shard_map/while/body/eval_jaxpr/fb,fr->br/dot_general | solution.py:14
  756.1 10.0 %fusion.40 = f32[8192,128]{1,0:T(8,128)} fusion(f32[8,128]{1,0:T(8,128)S(1)} %get-tuple-element.266, f32[128]{0:T(128)S(1)} %get-tuple-element.267, f32[8192]{0:T(1024)S(1)} %broadcast_multiply_fusion.8, f32[8,8,8192]{2,1,0:T(8,128)} %get-tuple-element.265, s32[]{:T(128)} %get-tuple-element.254), kind=kOutput, calls=%fused_computation.14.clone.1 | convolution fusion | flops 102760448 | bytes 4494336 | tf_op jit(solution)/shard_map/while/body/eval_jaxpr/fb,fr->br/dot_general | solution.py:14
  771.8 10.0 %fusion.40 = f32[8192,128]{1,0:T(8,128)} fusion(f32[8,128]{1,0:T(8,128)S(1)} %get-tuple-element.266, f32[128]{0:T(128)S(1)} %get-tuple-element.267, f32[8192]{0:T(1024)S(1)} %broadcast_multiply_fusion.8, f32[8,8,8192]{2,1,0:T(8,128)} %get-tuple-element.265, s32[]{:T(128)} %get-tuple-element.254), kind=kOutput, calls=%fused_computation.14.clone.1 | convolution fusion | flops 102760448 | bytes 4494336 | tf_op jit(solution)/shard_map/while/body/eval_jaxpr/fb,fr->br/dot_general | solution.py:14
  787.4 10.0 %fusion.40 = f32[8192,128]{1,0:T(8,128)} fusion(f32[8,128]{1,0:T(8,128)S(1)} %get-tuple-element.266, f32[128]{0:T(128)S(1)} %get-tuple-element.267, f32[8192]{0:T(1024)S(1)} %broadcast_multiply_fusion.8, f32[8,8,8192]{2,1,0:T(8,128)} %get-tuple-element.265, s32[]{:T(128)} %get-tuple-element.254), kind=kOutput, calls=%fused_computation.14.clone.1 | convolution fusion | flops 102760448 | bytes 4494336 | tf_op jit(solution)/shard_map/while/body/eval_jaxpr/fb,fr->br/dot_general | solution.py:14
  803.0 10.0 %fusion.40 = f32[8192,128]{1,0:T(8,128)} fusion(f32[8,128]{1,0:T(8,128)S(1)} %get-tuple-element.266, f32[128]{0:T(128)S(1)} %get-tuple-element.267, f32[8192]{0:T(1024)S(1)} %broadcast_multiply_fusion.8, f32[8,8,8192]{2,1,0:T(8,128)} %get-tuple-element.265, s32[]{:T(128)} %get-tuple-element.254), kind=kOutput, calls=%fused_computation.14.clone.1 | convolution fusion | flops 102760448 | bytes 4494336 | tf_op jit(solution)/shard_map/while/body/eval_jaxpr/fb,fr->br/dot_general | solution.py:14
  818.6 10.0 %fusion.40 = f32[8192,128]{1,0:T(8,128)} fusion(f32[8,128]{1,0:T(8,128)S(1)} %get-tuple-element.266, f32[128]{0:T(128)S(1)} %get-tuple-element.267, f32[8192]{0:T(1024)S(1)} %broadcast_multiply_fusion.8, f32[8,8,8192]{2,1,0:T(8,128)} %get-tuple-element.265, s32[]{:T(128)} %get-tuple-element.254), kind=kOutput, calls=%fused_computation.14.clone.1 | convolution fusion | flops 102760448 | bytes 4494336 | tf_op jit(solution)/shard_map/while/body/eval_jaxpr/fb,fr->br/dot_general | solution.py:14
  833.4 96.8 %psum.31 = f32[16]{0:T(128)S(1)} all-reduce(f32[16]{0:T(128)S(1)} %multiply_reduce_fusion), channel_id=1, replica_groups=mesh['row'=32,'col'=16] {'row','col'}, use_global_device_ids=true, to_apply=%region_14.15 | all-reduce | flops 16 | bytes 128 | tf_op jit(solution)/shard_map/psum | solution.py:61
  (84 shorter events, 121.9 us)
Async XLA Ops:
  7.2 130.1 %all-gather.4.cloned.1.call-start = ((), (), s32[]{:S(2)}) async-start(), calls=%async_computation | async-start | bytes 4202496 | tf_op jit(solution)/shard_map/all_gather | solution.py:57
  7.9 246.4 %all-gather.6.cloned.1.call-start = ((), (), s32[]{:S(2)}) async-start(), calls=%async_computation.1 | async-start | bytes 2101248 | tf_op jit(solution)/shard_map/all_gather | solution.py:45
  9.3 694.4 %all-gather.8.cloned.1.call-start = ((), (), s32[]{:S(2)}) async-start(), calls=%async_computation.2 | async-start | bytes 4202496 | tf_op jit(solution)/shard_map/all_gather | solution.py:57
  137.3 117.0 %copy-start = (f32[8,128]{1,0:T(8,128)S(1)}, f32[8,128]{1,0:T(8,128)}, u32[]{:S(2)}) copy-start(f32[8,128]{1,0:T(8,128)} %get-tuple-element.250) | copy-start | bytes 12292
  254.3 143.0 %copy-start.1 = (f32[16,128]{1,0:T(8,128)S(1)}, f32[16,128]{1,0:T(8,128)}, u32[]{:S(2)}) copy-start(f32[16,128]{1,0:T(8,128)} %param.10) | copy-start | bytes 24580
  254.3 143.0 %copy-start.3 = (f32[16]{0:T(128)S(1)}, f32[16]{0:T(128)}, u32[]{:S(2)}) copy-start(f32[16]{0:T(128)} %param.11) | copy-start | bytes 196
  708.2 125.0 %copy-start.2 = (f32[16,128]{1,0:T(8,128)S(1)}, f32[16,128]{1,0:T(8,128)}, u32[]{:S(2)}) copy-start(f32[16,128]{1,0:T(8,128)} %multiply_add_fusion.2) | copy-start | bytes 24580
Sparse Core Ops, SparseCore 0:
  12.2 124.9 all-gather.3
  142.0 112.1 all-gather.5
  588.7 114.8 all-gather.7
where the time goes:
time: 939 us; the launch traced here: 937 us
  waiting for transfers between devices  354 us (38%)
  blocking collectives  287 us (31%)
  matrix products  230 us (24%)
  local copies, waits for them, and re-layouts  32.3 us (3%)
  other arithmetic  19.8 us (2%)
  between operations  13.8 us (1%)
    all_gather x2, waiting for transfers between devices, on_device(): lax.all_gather(direction, ('row', 'col'), axis=1, tiled=True)  243 us
    psum x2, blocking collectives, squares(): return lax.psum(jnp.sum(residual * residual, axis=1), ('row', 'col'))  190 us
    dot_general x16, matrix products, block_terms(): inner_products = jnp.einsum('fb,fr->br', col_z, row_z, precision=exact_mode)  161 us
    all_gather x1, waiting for transfers between devices, on_device(): all_scaled = lax.all_gather(scaled, ('row', 'col'), axis=1, tiled=True)  110 us
    psum x1, blocking collectives, on_device(): curvature = lax.psum(jnp.sum(direction * image, axis=1), ('row', 'col'))  96.8 us
    dot_general x16, matrix products, block_terms(): jnp.dot(col_v, kernel, precision=exact_mode, preferred_element_type=jnp.f...  68.9 us
    dynamic_slice x8, local copies, waits for them, and re-layouts, kernel_terms(): accumulated, unused = lax.scan(advance, initial, (z_slabs, v_slabs))  21.2 us
  transfers between devices with their start and end apart: 3, of which 3 were waited for; matrix products, arithmetic and copies ran while one was open for 1% of the time, Pallas kernels for 0%

commit v1 on v0

v1 whole, which is shorter than its diff:
```python
import functools
import math

import jax
import jax.numpy as jnp
from jax import lax
from jax.experimental import pallas as pl
from jax.experimental.pallas import tpu as pltpu
from jax.sharding import PartitionSpec as P

LANES = 128
NFEAT = 8
NRHS = 16
FEATURE_ROWS = 64
ROOT_LOG2E = math.sqrt(math.log2(math.e))
STEP = 512
WIDE = 256


def pieces(value):
    high = value.astype(jnp.bfloat16).astype(jnp.float32)
    rest = value - high
    middle = rest.astype(jnp.bfloat16).astype(jnp.float32)
    low = (rest - middle).astype(jnp.bfloat16).astype(jnp.float32)
    return high, middle, low


def features(scaled, is_left):
    z = scaled * ROOT_LOG2E
    high, middle, low = pieces(z)
    norm_pieces = pieces(-0.5 * jnp.sum(z * z, axis=0, keepdims=True))
    row = lax.broadcasted_iota(jnp.int32, z.shape, 0)
    start = 0 if is_left else 3
    norms = jnp.where((row < 6) & ((row < start) | (row >= start + 3)), 1.0, 0.0)
    for place, piece in enumerate(norm_pieces):
        norms = jnp.where(row == start + place, piece, norms)
    if is_left:
        parts = [high, high, middle, middle, high, low]
    else:
        parts = [high, middle, high, middle, low, high]
    return jnp.concatenate(parts + [norms, jnp.zeros_like(z)], axis=0)


def dot(left, right):
    return lax.dot_general(left, right, (((1,), (0,)), ((), ())), preferred_element_type=jnp.float32)


def image_kernel(left_ref, vector_ref, right_ref, out_ref, left, right, vector, total):
    for block in range(right_ref.shape[0]):
        span = pl.ds(block * LANES, LANES)
        right[:, span] = features(right_ref[block], False).astype(jnp.bfloat16)
    for block in range(left_ref.shape[0]):
        span = pl.ds(block * LANES, LANES)
        left[span, :] = features(left_ref[block, :NFEAT, :], True).T.astype(jnp.bfloat16)
        vector[:, span] = jnp.concatenate(pieces(vector_ref[block]), axis=0).astype(jnp.bfloat16)
    total[...] = jnp.zeros_like(total)

    def advance(step, unused):
        offset = pl.multiple_of(step * STEP, STEP)
        left_block = left[pl.ds(offset, STEP), :]
        vector_block = vector[:, pl.ds(offset, STEP)]
        for place in range(right.shape[1] // WIDE):
            span = pl.ds(place * WIDE, WIDE)
            kernel = jnp.exp2(dot(left_block, right[:, span]))
            high = kernel.astype(jnp.bfloat16)
            low = (kernel - high.astype(jnp.float32)).astype(jnp.bfloat16)
            total[:, span] += dot(vector_block, high) + dot(vector_block, low)
        return unused

    lax.fori_loop(0, left.shape[0] // STEP, advance, 0)
    for block in range(right_ref.shape[0]):
        terms = total[:, pl.ds(block * LANES, LANES)]
        out_ref[block] = terms[:NRHS] + terms[NRHS : 2 * NRHS] + terms[2 * NRHS :]


def image_terms(left, vector, right):
    left_count, right_count = left.shape[0] * LANES, right.shape[0] * LANES
    vmem = pl.BlockSpec(memory_space=pltpu.VMEM)
    return pl.pallas_call(
        image_kernel,
        out_shape=jax.ShapeDtypeStruct((right.shape[0], NRHS, LANES), jnp.float32),
        in_specs=[vmem] * 3,
        out_specs=vmem,
        scratch_shapes=[
            pltpu.VMEM((left_count, FEATURE_ROWS), jnp.bfloat16),
            pltpu.VMEM((FEATURE_ROWS, right_count), jnp.bfloat16),
            pltpu.VMEM((3 * NRHS, left_count), jnp.bfloat16),
            pltpu.VMEM((3 * NRHS, right_count), jnp.float32),
        ],
        compiler_params=pltpu.CompilerParams(vmem_limit_bytes=40 << 20),
    )(left, vector, right)


def exchange(blocks, axis):
    return lax.all_to_all(blocks, axis, 0, 0, tiled=True)


def gather(block, axis, count):
    return exchange(jnp.broadcast_to(block[None], (count,) + block.shape), axis)


def tile_of(sums):
    stacked = jnp.stack(sums)
    return jnp.pad(stacked, ((0, 8 - stacked.shape[0]), (0, LANES - NRHS)))


def inner(left, right):
    return jnp.sum(left * right, axis=1)


def on_device(rows, cols, points, inverse_scale, targets, noise_var):
    scaled = points * inverse_scale[:, None]
    noise = noise_var[:, None]
    left = gather(jnp.concatenate([scaled, targets], axis=0), "row", rows)
    right = gather(scaled, "col", cols)

    partial = image_terms(left, left[:, NFEAT:], right)
    image = jnp.sum(exchange(partial, "col"), axis=0) + noise * targets

    sums = tile_of([inner(targets, targets), inner(targets, image)])
    gathered = gather(jnp.concatenate([image, sums], axis=0), "row", rows)
    partial = image_terms(left, gathered[:, :NRHS], right)
    sums = jnp.sum(gathered[:, NRHS:], axis=0)
    partial = jnp.concatenate([partial, jnp.broadcast_to(sums[None], (cols,) + sums.shape)], axis=1)
    reduced = jnp.sum(exchange(partial, "col"), axis=0)
    image_image = reduced[:NRHS] + noise * image

    norm_now, curvature = reduced[NRHS, :NRHS], reduced[NRHS + 1, :NRHS]
    step_size = (norm_now / curvature)[:, None]
    residual = targets - step_size * image
    residual_image = image - step_size * image_image
    sums = tile_of([inner(residual, residual), inner(residual, residual_image), inner(residual, image)])
    sums = jnp.sum(gather(sums, "col", cols), axis=0)
    sums = jnp.sum(gather(sums, "row", rows), axis=0)
    norm_next = sums[0, :NRHS]
    ratio = norm_next / norm_now
    next_curvature = sums[1, :NRHS] + ratio * (2.0 * sums[2, :NRHS] + ratio * curvature)
    next_step = (norm_next / next_curvature)[:, None]
    ratio = ratio[:, None]
    solution = step_size * targets + next_step * (residual + ratio * targets)
    residual = residual - next_step * (residual_image + ratio * image)
    return (solution, residual)


def solution(mesh):
    return jax.shard_map(
        functools.partial(on_device, mesh.shape["row"], mesh.shape["col"]),
        mesh=mesh,
        in_specs=(P(None, ("row", "col")), P(), P(None, ("row", "col")), P()),
        out_specs=(P(None, ("row", "col")), P(None, ("row", "col"))),
        check_vma=False,
    )
```

time: 939 us -> 144 us (0.15)
  waiting for transfers between devices: 354 us -> 7.79 us
  matrix products: 230 us -> 0 us
  blocking collectives: 287 us -> 92.8 us
  local copies, waits for them, and re-layouts: 32.3 us -> 1.38 us
  Pallas kernels: 0 us -> 25.7 us
  other arithmetic: 19.8 us -> 2.05 us
  between operations: 13.8 us -> 0.73 us
  starting transfers between devices: 0.12 us -> 12.8 us
    all_gather x3 -> x0, waiting for transfers between devices: 353 us -> none  [the longest x2 243 us: on_device(): lax.all_gather(direction, ('row', 'col'), axis=1, tiled=True)]
    psum x3 -> x0, blocking collectives: 287 us -> none  [the longest x2 190 us: squares(): return lax.psum(jnp.sum(residual * residual, axis=1), ('row', 'col'))]
    dot_general x32 -> x0, matrix products: 230 us -> none  [the longest x16 161 us: block_terms(): inner_products = jnp.einsum('fb,fr->br', col_z, row_z, precision=exact_mode)]
    all_to_all x0 -> x6, blocking collectives: none -> 92.8 us  [exchange(): return lax.all_to_all(blocks, axis, 0, 0, tiled=True)]
    pallas_call x0 -> x2, Pallas kernels: none -> 25.7 us  [image_terms(): pl.pallas_call(image_kernel, out_shape=jax.ShapeDtypeStruct((right.shape[...]
    dynamic_slice x8 -> x0, local copies, waits for them, and re-layouts: 21.2 us -> none  [kernel_terms(): accumulated, unused = lax.scan(advance, initial, (z_slabs, v_slabs))]
    reduce_sum x20 -> x7, other arithmetic: 18.4 us -> 0.53 us  [the longest x2 0.4 us: inner(): return jnp.sum(left * right, axis=1)]
    all_to_all x0 -> x1, starting transfers between devices: none -> 12.8 us  [exchange(): return lax.all_to_all(blocks, axis, 0, 0, tiled=True)]
  transfers between devices with their start and end apart: 3 -> 1, of which waited for: 3 -> 1; matrix products, arithmetic and copies ran while one was open for 1% -> 0% of each run, Pallas kernels for 0% -> 0%
where the time goes in v1:
time: 144 us; the launch traced here: 143 us
  blocking collectives  92.8 us (64%)
  Pallas kernels  25.7 us (18%)
  starting transfers between devices  12.8 us (9%)
  waiting for transfers between devices  7.79 us (5%)
  other arithmetic  2.05 us (1%)
    all_to_all x6, blocking collectives, exchange(): return lax.all_to_all(blocks, axis, 0, 0, tiled=True)  92.8 us
    pallas_call x2, Pallas kernels, image_terms(): pl.pallas_call(image_kernel, out_shape=jax.ShapeDtypeStruct((right.shape[...  25.7 us
    all_to_all x1, starting transfers between devices, exchange(): return lax.all_to_all(blocks, axis, 0, 0, tiled=True)  12.8 us
    all_to_all x1, waiting for transfers between devices, exchange(): return lax.all_to_all(blocks, axis, 0, 0, tiled=True)  7.79 us
  transfers between devices with their start and end apart: 1, of which 1 were waited for; matrix products, arithmetic and copies ran while one was open for 0% of the time, Pallas kernels for 0%

profile of v1, /device:TPU:1, one launch (start us, length us, event | category | flops | bytes accessed | tf_op | source)
XLA Modules:
  0.0 143.2 jit_solution(9735140855146075923)
XLA Ops:
  0.6 0.0 copy-start
  0.6 0.8 broadcast_multiply_fusion
  1.4 0.0 copy-done
  1.4 24.1 %all_to_all.35.left_ref = f32[32,24,128]{2,1,0:T(8,128)S(1)} all-to-all(f32[32,24,128]{2,1,0:T(8,128)S(1)} %broadcast_in_dim.12), channel_id=1, replica_groups=mesh['row'=32,'col'=16] {'row'}, dimensions={0} | all-to-all | bytes 786432 | tf_op jit(solution)/shard_map/all_to_all | solution.py:95
  25.5 0.6 broadcast_in_dim.13
  26.2 12.8 %all-to-all-start.1 = ((f32[16,8,128]{2,1,0:T(8,128)}), f32[16,8,128]{2,1,0:T(8,128)S(1)}, u32[]{:S(2)}, u32[]{:S(2)}) async-start(f32[16,8,128]{2,1,0:T(8,128)} %broadcast_in_dim.13), calls=%async_computation.1 | async-start | bytes 131072 | tf_op jit(solution)/shard_map/all_to_all | solution.py:95
  39.0 7.8 %all-to-all-done.1.right_ref = f32[16,8,128]{2,1,0:T(8,128)S(1)} async-done(((f32[16,8,128]{2,1,0:T(8,128)}), f32[16,8,128]{2,1,0:T(8,128)S(1)}, u32[]{:S(2)}, u32[]{:S(2)}) %all-to-all-start.1) | async-done | bytes 65568 | tf_op jit(solution)/shard_map/all_to_all | solution.py:95
  46.8 12.8 %shard_map.59 = f32[16,16,128]{2,1,0:T(8,128)S(1)} custom-call(f32[32,24,128]{2,1,0:T(8,128)S(1)} %all_to_all.35.left_ref, f32[32,16,128]{2,1,0:T(8,128)S(1)} %slice.36.vector_ref, f32[16,8,128]{2,1,0:T(8,128)S(1)} %all-to-all-done.1.right_ref), custom_call_target="tpu_custom_call" | custom-call | tf_op jit(solution)/shard_map/pallas_call | solution.py:79
  59.6 11.8 %all_to_all.36 = f32[16,16,128]{2,1,0:T(8,128)S(1)} all-to-all(f32[16,16,128]{2,1,0:T(8,128)S(1)} %shard_map.59), channel_id=1, replica_groups=mesh['row'=32,'col'=16] {'col'}, dimensions={0} | all-to-all | bytes 262144 | tf_op jit(solution)/shard_map/all_to_all | solution.py:95
  71.4 0.0 copy-start.1
  71.4 0.6 copy-done.1
  72.1 0.2 multiply_reduce_fusion.4
  72.3 18.5 %all_to_all.37 = f32[32,24,128]{2,1,0:T(8,128)S(1)} all-to-all(f32[32,24,128]{2,1,0:T(8,128)S(1)} %broadcast_in_dim.14), channel_id=1, replica_groups=mesh['row'=32,'col'=16] {'row'}, dimensions={0} | all-to-all | bytes 786432 | tf_op jit(solution)/shard_map/all_to_all | solution.py:95
  90.8 12.8 %shard_map.60 = f32[16,16,128]{2,1,0:T(8,128)S(1)} custom-call(f32[32,24,128]{2,1,0:T(8,128)S(1)} %all_to_all.35.left_ref, f32[32,16,128]{2,1,0:T(8,128)S(1)} %slice.37.vector_ref, f32[16,8,128]{2,1,0:T(8,128)S(1)} %all-to-all-done.1.right_ref), custom_call_target="tpu_custom_call" | custom-call | tf_op jit(solution)/shard_map/pallas_call | solution.py:79
  103.7 14.0 %all_to_all.38 = f32[16,24,128]{2,1,0:T(8,128)S(1)} all-to-all(f32[16,24,128]{2,1,0:T(8,128)S(1)} %pad_maximum_fusion), channel_id=1, replica_groups=mesh['row'=32,'col'=16] {'col'}, dimensions={0} | all-to-all | bytes 393216 | tf_op jit(solution)/shard_map/all_to_all | solution.py:95
  117.8 0.2 multiply_reduce_fusion.2
  118.0 10.5 %all_to_all.39 = f32[16,8,128]{2,1,0:T(8,128)S(1)} all-to-all(f32[16,8,128]{2,1,0:T(8,128)S(1)} %broadcast_in_dim.16), channel_id=1, replica_groups=mesh['row'=32,'col'=16] {'col'}, dimensions={0} | all-to-all | bytes 131072 | tf_op jit(solution)/shard_map/all_to_all | solution.py:95
  128.5 14.0 %all_to_all.40 = f32[32,8,128]{2,1,0:T(8,128)S(1)} all-to-all(f32[32,8,128]{2,1,0:T(8,128)S(1)} %broadcast_in_dim.17), channel_id=1, replica_groups=mesh['row'=32,'col'=16] {'row'}, dimensions={0} | all-to-all | bytes 262144 | tf_op jit(solution)/shard_map/all_to_all | solution.py:95
  142.5 0.7 multiply_subtract_fusion
  (19 shorter events, 0.3 us)
Async XLA Ops:
  0.6 0.8 copy-start
  26.2 20.6 %all-to-all-start.1 = ((f32[16,8,128]{2,1,0:T(8,128)}), f32[16,8,128]{2,1,0:T(8,128)S(1)}, u32[]{:S(2)}, u32[]{:S(2)}) async-start(f32[16,8,128]{2,1,0:T(8,128)} %broadcast_in_dim.13), calls=%async_computation.1 | async-start | bytes 131072 | tf_op jit(solution)/shard_map/all_to_all | solution.py:95
  71.4 0.7 copy-start.1

commit v2 on v1

v2 whole, which is shorter than its diff:
```python
import functools
import math

import jax
import jax.numpy as jnp
from jax import lax
from jax.experimental import pallas as pl
from jax.experimental.pallas import tpu as pltpu
from jax.sharding import PartitionSpec as P

LANES = 128
NFEAT = 8
NRHS = 16
SUMS = 8
FEATURE_ROWS = 64
ROOT_LOG2E = math.sqrt(math.log2(math.e))
STEP = 512
WIDE = 256


def pieces(value):
    high = value.astype(jnp.bfloat16).astype(jnp.float32)
    rest = value - high
    middle = rest.astype(jnp.bfloat16).astype(jnp.float32)
    low = (rest - middle).astype(jnp.bfloat16).astype(jnp.float32)
    return high, middle, low


def features(scaled, is_left):
    z = scaled * ROOT_LOG2E
    high, middle, low = pieces(z)
    norm_pieces = pieces(-0.5 * jnp.sum(z * z, axis=0, keepdims=True))
    row = lax.broadcasted_iota(jnp.int32, z.shape, 0)
    start = 0 if is_left else 3
    norms = jnp.where((row < 6) & ((row < start) | (row >= start + 3)), 1.0, 0.0)
    for place, piece in enumerate(norm_pieces):
        norms = jnp.where(row == start + place, piece, norms)
    if is_left:
        parts = [high, high, middle, middle, high, low]
    else:
        parts = [high, middle, high, middle, low, high]
    return jnp.concatenate(parts + [norms, jnp.zeros_like(z)], axis=0)


def dot(left, right):
    return lax.dot_general(left, right, (((1,), (0,)), ((), ())), preferred_element_type=jnp.float32)


def write_features(left_ref, right_ref, left, right):
    for block in range(right_ref.shape[0]):
        span = pl.ds(block * LANES, LANES)
        right[:, span] = features(right_ref[block, :NFEAT, :], False).astype(jnp.bfloat16)
    for block in range(left_ref.shape[0]):
        span = pl.ds(block * LANES, LANES)
        left[span, :] = features(left_ref[block, :NFEAT, :], True).T.astype(jnp.bfloat16)


def write_vector(block, value, vector):
    span = pl.ds(block * LANES, LANES)
    vector[:, span] = jnp.concatenate(pieces(value), axis=0).astype(jnp.bfloat16)


def multiply(left, right, vector, total):
    total[...] = jnp.zeros_like(total)

    def advance(step, unused):
        offset = pl.multiple_of(step * STEP, STEP)
        left_block = left[pl.ds(offset, STEP), :]
        vector_block = vector[:, pl.ds(offset, STEP)]
        for place in range(right.shape[1] // WIDE):
            span = pl.ds(place * WIDE, WIDE)
            kernel = jnp.exp2(dot(left_block, right[:, span]))
            high = kernel.astype(jnp.bfloat16)
            low = (kernel - high.astype(jnp.float32)).astype(jnp.bfloat16)
            total[:, span] += dot(vector_block, high) + dot(vector_block, low)
        return unused

    lax.fori_loop(0, left.shape[0] // STEP, advance, 0)


def block_terms(total, block):
    terms = total[:, pl.ds(block * LANES, LANES)]
    return terms[:NRHS] + terms[NRHS : 2 * NRHS] + terms[2 * NRHS :]


def write_sums(products, out_ref):
    empty = jnp.zeros((LANES - NRHS * len(products), LANES), jnp.float32)
    turned = jnp.concatenate(products + [empty], axis=0).T
    row = jnp.sum(turned, axis=0, keepdims=True)
    for block in range(out_ref.shape[0]):
        out_ref[block, NRHS:, :] = jnp.broadcast_to(row, (SUMS, LANES))


def first_kernel(left_ref, right_ref, out_ref, left, right, vector, total):
    write_features(left_ref, right_ref, left, right)
    square = jnp.zeros((NRHS, LANES), jnp.float32)
    for block in range(left_ref.shape[0]):
        value = left_ref[block, NFEAT:, :]
        write_vector(block, value, vector)
        square += value * value
    multiply(left, right, vector, total)
    product = jnp.zeros((NRHS, LANES), jnp.float32)
    for block in range(right_ref.shape[0]):
        terms = block_terms(total, block)
        out_ref[block, :NRHS, :] = terms
        product += terms * right_ref[block, NFEAT:, :]
    write_sums([product, square], out_ref)


def second_kernel(
    left_ref, right_ref, left_image_ref, right_image_ref, noise_ref, out_ref, left, right, vector, total
):
    row = jnp.zeros((SUMS, LANES), jnp.float32)
    for block in range(left_ref.shape[0]):
        row += left_image_ref[block, NRHS:, :]
    product = jnp.broadcast_to(row[:1], (LANES, LANES)).T[:NRHS]
    norm = jnp.broadcast_to(left_image_ref[0, NRHS : NRHS + 1, :], (LANES, LANES)).T[NRHS : 2 * NRHS]
    step_size = norm / (product + noise_ref[...] * norm)

    write_features(left_ref, right_ref, left, right)
    square = jnp.zeros((NRHS, LANES), jnp.float32)
    crossed = jnp.zeros((NRHS, LANES), jnp.float32)
    for block in range(left_ref.shape[0]):
        image = left_image_ref[block, :NRHS, :]
        residual = left_ref[block, NFEAT:, :] - step_size * image
        write_vector(block, residual, vector)
        square += residual * residual
        crossed += residual * image
    multiply(left, right, vector, total)
    product = jnp.zeros((NRHS, LANES), jnp.float32)
    for block in range(right_ref.shape[0]):
        terms = block_terms(total, block)
        out_ref[block, :NRHS, :] = terms
        product += terms * (right_ref[block, NFEAT:, :] - step_size * right_image_ref[block])
    write_sums([product, square, crossed], out_ref)


def call_kernel(body, left, right, *others):
    left_count, right_count = left.shape[0] * LANES, right.shape[0] * LANES
    vmem = pl.BlockSpec(memory_space=pltpu.VMEM)
    return pl.pallas_call(
        body,
        out_shape=jax.ShapeDtypeStruct((right.shape[0], NRHS + SUMS, LANES), jnp.float32),
        in_specs=[vmem] * (2 + len(others)),
        out_specs=vmem,
        scratch_shapes=[
            pltpu.VMEM((left_count, FEATURE_ROWS), jnp.bfloat16),
            pltpu.VMEM((FEATURE_ROWS, right_count), jnp.bfloat16),
            pltpu.VMEM((3 * NRHS, left_count), jnp.bfloat16),
            pltpu.VMEM((3 * NRHS, right_count), jnp.float32),
        ],
        compiler_params=pltpu.CompilerParams(vmem_limit_bytes=40 << 20),
    )(left, right, *others)


def exchange(blocks, axis):
    return lax.all_to_all(blocks, axis, 0, 0, tiled=True)


def gather(block, axis, count):
    return exchange(jnp.broadcast_to(block[None], (count,) + block.shape), axis)


def on_device(rows, points, inverse_scale, targets, noise_var):
    noise = noise_var[:, None]
    known = jnp.concatenate([points * inverse_scale[:, None], targets], axis=0)
    left = gather(known, "row", rows)
    right = lax.all_gather(known, "col", axis=0)

    reduced = jnp.sum(exchange(call_kernel(first_kernel, left, right), "col"), axis=0)
    image = reduced[:NRHS] + noise * targets
    norm_now = reduced[NRHS, NRHS : 2 * NRHS]

    left_image = gather(jnp.concatenate([image, reduced[NRHS:]], axis=0), "row", rows)
    right_image = lax.all_gather(image, "col", axis=0)
    wide_noise = jnp.broadcast_to(noise, (NRHS, LANES))
    partial = call_kernel(second_kernel, left, right, left_image, right_image, wide_noise)
    curvature = jnp.sum(left_image[:, NRHS, :NRHS], axis=0) + noise_var * norm_now
    step_size = (norm_now / curvature)[:, None]
    residual = targets - step_size * image

    reduced = jnp.sum(exchange(partial, "col"), axis=0)
    norm_next = reduced[NRHS, NRHS : 2 * NRHS]
    crossed = reduced[NRHS, 2 * NRHS : 3 * NRHS]
    sums = gather(reduced[NRHS:], "row", rows)
    residual_curvature = jnp.sum(sums[:, 0, :NRHS], axis=0) + noise_var * norm_next
    ratio = norm_next / norm_now
    next_curvature = residual_curvature + ratio * (2.0 * crossed + ratio * curvature)
    next_step = (norm_next / next_curvature)[:, None]
    ratio = ratio[:, None]
    residual_image = reduced[:NRHS] + noise * residual
    solution = step_size * targets + next_step * (residual + ratio * targets)
    residual = residual - next_step * (residual_image + ratio * image)
    return (solution, residual)


def solution(mesh):
    return jax.shard_map(
        functools.partial(on_device, mesh.shape["row"]),
        mesh=mesh,
        in_specs=(P(None, ("row", "col")), P(), P(None, ("row", "col")), P()),
        out_specs=(P(None, ("row", "col")), P(None, ("row", "col"))),
        check_vma=False,
    )
```

time: 144 us -> 139 us (0.965)
  blocking collectives: 92.8 us -> 67.8 us
  starting transfers between devices: 12.8 us -> 29.5 us
  waiting for transfers between devices: 7.79 us -> 9.86 us
  local copies, waits for them, and re-layouts: 1.38 us -> 2.9 us
    all_to_all x6 -> x2, blocking collectives: 92.8 us -> 28.5 us  [exchange(): return lax.all_to_all(blocks, axis, 0, 0, tiled=True)]
    all_gather x0 -> x2, blocking collectives: none -> 39.3 us  [the longest x1 24.5 us: on_device(): right = lax.all_gather(known, 'col', axis=0)]
    all_to_all x1 -> x3, starting transfers between devices: 12.8 us -> 29.5 us  [exchange(): return lax.all_to_all(blocks, axis, 0, 0, tiled=True)]
    all_to_all x1 -> x3, waiting for transfers between devices: 7.79 us -> 9.86 us  [exchange(): return lax.all_to_all(blocks, axis, 0, 0, tiled=True)]
    broadcast_in_dim x5 -> x3, local copies, waits for them, and re-layouts: 0.7 us -> 2.18 us  [gather(): return exchange(jnp.broadcast_to(block[None], (count,) + block.shape), axis)]
  transfers between devices with their start and end apart: 1 -> 3, of which waited for: 1 -> 1; matrix products, arithmetic and copies ran while one was open for 0% -> 0% of each run, Pallas kernels for 0% -> 0%
where the time goes in v2:
time: 139 us
  blocking collectives  67.8 us (49%)
  starting transfers between devices  29.5 us (21%)
  Pallas kernels  26.1 us (19%)
  waiting for transfers between devices  9.86 us (7%)
  local copies, waits for them, and re-layouts  2.9 us (2%)
  other arithmetic  1.76 us (1%)
    all_to_all x3, starting transfers between devices, exchange(): return lax.all_to_all(blocks, axis, 0, 0, tiled=True)  29.5 us
    all_to_all x2, blocking collectives, exchange(): return lax.all_to_all(blocks, axis, 0, 0, tiled=True)  28.5 us
    pallas_call x2, Pallas kernels, call_kernel(): pl.pallas_call(body, out_shape=jax.ShapeDtypeStruct((right.shape[0], NRHS...  26.1 us
    all_gather x1, blocking collectives, on_device(): right = lax.all_gather(known, 'col', axis=0)  24.5 us
    all_gather x1, blocking collectives, on_device(): right_image = lax.all_gather(image, 'col', axis=0)  14.8 us
    all_to_all x3, waiting for transfers between devices, exchange(): return lax.all_to_all(blocks, axis, 0, 0, tiled=True)  9.86 us
  transfers between devices with their start and end apart: 3, of which 1 were waited for; matrix products, arithmetic and copies ran while one was open for 0% of the time, Pallas kernels for 0%

profile of v2, /device:TPU:1, one launch (start us, length us, event | category | flops | bytes accessed | tf_op | source)
XLA Modules:
  0.0 138.7 jit_solution(12664438660837890816)
XLA Ops:
  0.6 0.8 broadcast_multiply_fusion
  1.4 0.8 broadcast_in_dim.8
  2.2 10.5 %all-to-all-start = ((f32[32,24,128]{2,1,0:T(8,128)}), f32[32,24,128]{2,1,0:T(8,128)S(1)}, u32[]{:S(2)}, u32[]{:S(2)}) async-start(f32[32,24,128]{2,1,0:T(8,128)} %broadcast_in_dim.8), calls=%async_computation | async-start | bytes 786432 | tf_op jit(solution)/shard_map/all_to_all | solution.py:157
  12.7 24.5 %all-gather = f32[384,128]{1,0:T(8,128)S(1)} all-gather(f32[24,128]{1,0:T(8,128)S(1)} %pad_maximum_fusion), channel_id=2, replica_groups=mesh['row'=32,'col'=16] {'col'}, dimensions={0}, use_global_device_ids=true | all-gather | bytes 208896 | tf_op jit(solution)/shard_map/all_gather | solution.py:168
  37.2 0.0 all-to-all-done.left_ref
  37.2 13.0 %shard_map.59 = f32[16,24,128]{2,1,0:T(8,128)S(1)} custom-call(f32[32,24,128]{2,1,0:T(8,128)S(1)} %all-to-all-done.left_ref, f32[16,24,128]{2,1,0:T(8,128)S(1)} %bitcast.26), custom_call_target="tpu_custom_call" | custom-call | tf_op jit(solution)/shard_map/pallas_call | solution.py:141
  50.1 13.1 %all_to_all.25 = f32[16,24,128]{2,1,0:T(8,128)S(1)} all-to-all(f32[16,24,128]{2,1,0:T(8,128)S(1)} %shard_map.59), channel_id=1, replica_groups=mesh['row'=32,'col'=16] {'col'}, dimensions={0} | all-to-all | bytes 393216 | tf_op jit(solution)/shard_map/all_to_all | solution.py:157
  63.2 0.0 copy-start.1
  63.3 0.6 copy-done.1
  63.9 0.1 slice_add_fusion.1
  64.0 0.8 broadcast_in_dim.10
  64.7 9.5 %all-to-all-start.2 = ((f32[32,24,128]{2,1,0:T(8,128)}), f32[32,24,128]{2,1,0:T(8,128)S(1)}, u32[]{:S(2)}, u32[]{:S(2)}) async-start(f32[32,24,128]{2,1,0:T(8,128)} %broadcast_in_dim.10), calls=%async_computation.2 | async-start | bytes 786432 | tf_op jit(solution)/shard_map/all_to_all | solution.py:157
  74.2 14.8 %all-gather.1 = f32[256,128]{1,0:T(8,128)S(1)} all-gather(f32[16,128]{1,0:T(8,128)S(1)} %slice_add_fusion.1), channel_id=3, replica_groups=mesh['row'=32,'col'=16] {'col'}, dimensions={0}, use_global_device_ids=true | all-gather | bytes 139264 | tf_op jit(solution)/shard_map/all_gather | solution.py:175
  89.1 0.0 all-to-all-done.2.left_image_ref
  89.1 0.1 mul.84.noise_ref
  89.1 13.2 %shard_map.60 = f32[16,24,128]{2,1,0:T(8,128)S(1)} custom-call(f32[32,24,128]{2,1,0:T(8,128)S(1)} %all-to-all-done.left_ref, f32[16,24,128]{2,1,0:T(8,128)S(1)} %bitcast.27, f32[32,24,128]{2,1,0:T(8,128)S(1)} %all-to-all-done.2.left_image_ref, f32[16,16,128]{2,1,0:T(8,128)S(1)} %bitcast.28, f32[16,128]{1,0:T(8,128)S(1)} %mul.84.noise_ref), custom_call_target="tpu_custom_call" | custom-call | tf_op jit(solution)/shard_map/pallas_call | solution.py:141
  102.3 15.5 %all_to_all.26 = f32[16,24,128]{2,1,0:T(8,128)S(1)} all-to-all(f32[16,24,128]{2,1,0:T(8,128)S(1)} %shard_map.60), channel_id=1, replica_groups=mesh['row'=32,'col'=16] {'col'}, dimensions={0} | all-to-all | bytes 393216 | tf_op jit(solution)/shard_map/all_to_all | solution.py:157
  117.8 0.6 broadcast_in_dim.11
  118.5 9.5 %all-to-all-start.4 = ((f32[32,8,128]{2,1,0:T(8,128)}), f32[32,8,128]{2,1,0:T(8,128)S(1)}, u32[]{:S(2)}, u32[]{:S(2)}) async-start(f32[32,8,128]{2,1,0:T(8,128)} %broadcast_in_dim.11), calls=%async_computation.4 | async-start | bytes 262144 | tf_op jit(solution)/shard_map/all_to_all | solution.py:157
  128.0 0.1 slice_reduce_fusion.1
  128.0 9.9 %all-to-all-done.4 = f32[32,8,128]{2,1,0:T(8,128)S(1)} async-done(((f32[32,8,128]{2,1,0:T(8,128)}), f32[32,8,128]{2,1,0:T(8,128)S(1)}, u32[]{:S(2)}, u32[]{:S(2)}) %all-to-all-start.4) | async-done | bytes 131104 | tf_op jit(solution)/shard_map/all_to_all | solution.py:157
  137.9 0.1 slice_reduce_fusion
  137.9 0.1 add_divide_fusion
  138.0 0.7 fusion.2
  (8 shorter events, 0.1 us)
Async XLA Ops:
  0.6 0.8 copy-start
  2.2 35.0 %all-to-all-start = ((f32[32,24,128]{2,1,0:T(8,128)}), f32[32,24,128]{2,1,0:T(8,128)S(1)}, u32[]{:S(2)}, u32[]{:S(2)}) async-start(f32[32,24,128]{2,1,0:T(8,128)} %broadcast_in_dim.8), calls=%async_computation | async-start | bytes 786432 | tf_op jit(solution)/shard_map/all_to_all | solution.py:157
  63.2 0.7 copy-start.1
  64.7 24.3 %all-to-all-start.2 = ((f32[32,24,128]{2,1,0:T(8,128)}), f32[32,24,128]{2,1,0:T(8,128)S(1)}, u32[]{:S(2)}, u32[]{:S(2)}) async-start(f32[32,24,128]{2,1,0:T(8,128)} %broadcast_in_dim.10), calls=%async_computation.2 | async-start | bytes 786432 | tf_op jit(solution)/shard_map/all_to_all | solution.py:157
  118.5 19.4 %all-to-all-start.4 = ((f32[32,8,128]{2,1,0:T(8,128)}), f32[32,8,128]{2,1,0:T(8,128)S(1)}, u32[]{:S(2)}, u32[]{:S(2)}) async-start(f32[32,8,128]{2,1,0:T(8,128)} %broadcast_in_dim.11), calls=%async_computation.4 | async-start | bytes 262144 | tf_op jit(solution)/shard_map/all_to_all | solution.py:157

commit v3 on v1

--- a/solution.py
+++ b/solution.py
@@ -11,10 +11,12 @@
 LANES = 128
 NFEAT = 8
 NRHS = 16
+SUMS = 8
 FEATURE_ROWS = 64
 ROOT_LOG2E = math.sqrt(math.log2(math.e))
 STEP = 512
 WIDE = 256
+VMEM_LIMIT = 16 << 20
 
 
 def pieces(value):
@@ -45,50 +47,99 @@
     return lax.dot_general(left, right, (((1,), (0,)), ((), ())), preferred_element_type=jnp.float32)
 
 
-def image_kernel(left_ref, vector_ref, right_ref, out_ref, left, right, vector, total):
+def split_vector(value_of, vector):
+    for block in range(vector.shape[1] // LANES):
+        span = pl.ds(block * LANES, LANES)
+        vector[:, span] = jnp.concatenate(pieces(value_of(block)), axis=0).astype(jnp.bfloat16)
+
+
+def write_terms(total, out_ref):
+    for block in range(out_ref.shape[0]):
+        terms = total[:, pl.ds(block * LANES, LANES)]
+        out_ref[block, :NRHS, :] = terms[:NRHS] + terms[NRHS : 2 * NRHS] + terms[2 * NRHS :]
+
+
+def first_kernel(left_ref, right_ref, out_ref, high_ref, low_ref, left, right, vector, total):
     for block in range(right_ref.shape[0]):
         span = pl.ds(block * LANES, LANES)
         right[:, span] = features(right_ref[block], False).astype(jnp.bfloat16)
     for block in range(left_ref.shape[0]):
         span = pl.ds(block * LANES, LANES)
         left[span, :] = features(left_ref[block, :NFEAT, :], True).T.astype(jnp.bfloat16)
-        vector[:, span] = jnp.concatenate(pieces(vector_ref[block]), axis=0).astype(jnp.bfloat16)
+    split_vector(lambda block: left_ref[block, NFEAT:, :], vector)
     total[...] = jnp.zeros_like(total)
 
     def advance(step, unused):
-        offset = pl.multiple_of(step * STEP, STEP)
-        left_block = left[pl.ds(offset, STEP), :]
-        vector_block = vector[:, pl.ds(offset, STEP)]
+        rows = pl.ds(pl.multiple_of(step * STEP, STEP), STEP)
+        left_block = left[rows, :]
+        vector_block = vector[:, rows]
         for place in range(right.shape[1] // WIDE):
             span = pl.ds(place * WIDE, WIDE)
             kernel = jnp.exp2(dot(left_block, right[:, span]))
             high = kernel.astype(jnp.bfloat16)
             low = (kernel - high.astype(jnp.float32)).astype(jnp.bfloat16)
+            high_ref[rows, span] = high
+            low_ref[rows, span] = low
             total[:, span] += dot(vector_block, high) + dot(vector_block, low)
         return unused
 
     lax.fori_loop(0, left.shape[0] // STEP, advance, 0)
-    for block in range(right_ref.shape[0]):
-        terms = total[:, pl.ds(block * LANES, LANES)]
-        out_ref[block] = terms[:NRHS] + terms[NRHS : 2 * NRHS] + terms[2 * NRHS :]
+    write_terms(total, out_ref)
 
 
-def image_terms(left, vector, right):
+def second_kernel(left_ref, image_ref, high_ref, low_ref, out_ref, vector, total):
+    split_vector(lambda block: image_ref[block], vector)
+    for place in range(total.shape[1] // WIDE):
+        span = pl.ds(place * WIDE, WIDE)
+        total[:, span] = dot(vector[...], high_ref[:, span]) + dot(vector[...], low_ref[:, span])
+    write_terms(total, out_ref)
+    square = jnp.zeros((NRHS, LANES), jnp.float32)
+    product = jnp.zeros((NRHS, LANES), jnp.float32)
+    for block in range(left_ref.shape[0]):
+        target = left_ref[block, NFEAT:, :]
+        square += target * target
+        product += target * image_ref[block]
+    empty = jnp.zeros((LANES - 2 * NRHS, LANES), jnp.float32)
+    turned = jnp.concatenate([square, product, empty], axis=0).T
+    row = jnp.sum(turned, axis=0, keepdims=True)
+    for block in range(out_ref.shape[0]):
+        out_ref[block, NRHS:, :] = jnp.broadcast_to(row, (SUMS, LANES))
+
+
+VMEM_BLOCK = pl.BlockSpec(memory_space=pltpu.VMEM)
+
+
+def first_product(left, right):
     left_count, right_count = left.shape[0] * LANES, right.shape[0] * LANES
-    vmem = pl.BlockSpec(memory_space=pltpu.VMEM)
+    kept = pltpu.VMEM((left_count, right_count), jnp.bfloat16)
     return pl.pallas_call(
-        image_kernel,
-        out_shape=jax.ShapeDtypeStruct((right.shape[0], NRHS, LANES), jnp.float32),
-        in_specs=[vmem] * 3,
-        out_specs=vmem,
+        first_kernel,
+        out_shape=[jax.ShapeDtypeStruct((right.shape[0], NRHS, LANES), jnp.float32), kept, kept],
+        in_specs=[VMEM_BLOCK] * 2,
+        out_specs=[VMEM_BLOCK] * 3,
         scratch_shapes=[
             pltpu.VMEM((left_count, FEATURE_ROWS), jnp.bfloat16),
             pltpu.VMEM((FEATURE_ROWS, right_count), jnp.bfloat16),
             pltpu.VMEM((3 * NRHS, left_count), jnp.bfloat16),
             pltpu.VMEM((3 * NRHS, right_count), jnp.float32),
         ],
-        compiler_params=pltpu.CompilerParams(vmem_limit_bytes=40 << 20),
-    )(left, vector, right)
+        compiler_params=pltpu.CompilerParams(vmem_limit_bytes=VMEM_LIMIT),
+    )(left, right)
+
+
+def second_product(left, image, high, low):
+    left_count, right_count = high.shape
+    return pl.pallas_call(
+        second_kernel,
+        out_shape=jax.ShapeDtypeStruct((right_count // LANES, NRHS + SUMS, LANES), jnp.float32),
+        in_specs=[VMEM_BLOCK] * 4,
+        out_specs=VMEM_BLOCK,
+        scratch_shapes=[
+            pltpu.VMEM((3 * NRHS, left_count), jnp.bfloat16),
+            pltpu.VMEM((3 * NRHS, right_count), jnp.float32),
+        ],
+        compiler_params=pltpu.CompilerParams(vmem_limit_bytes=VMEM_LIMIT),
+    )(left, image, high, low)
 
 
 def exchange(blocks, axis):
@@ -101,7 +152,7 @@
 
 def tile_of(sums):
     stacked = jnp.stack(sums)
-    return jnp.pad(stacked, ((0, 8 - stacked.shape[0]), (0, LANES - NRHS)))
+    return jnp.pad(stacked, ((0, SUMS - stacked.shape[0]), (0, LANES - NRHS)))
 
 
 def inner(left, right):
@@ -109,23 +160,18 @@
 
 
 def on_device(rows, cols, points, inverse_scale, targets, noise_var):
+    noise = noise_var[:, None]
     scaled = points * inverse_scale[:, None]
-    noise = noise_var[:, None]
     left = gather(jnp.concatenate([scaled, targets], axis=0), "row", rows)
-    right = gather(scaled, "col", cols)
+    right = lax.all_gather(scaled, "col", axis=0)
 
-    partial = image_terms(left, left[:, NFEAT:], right)
+    partial, high, low = first_product(left, right)
     image = jnp.sum(exchange(partial, "col"), axis=0) + noise * targets
-
-    sums = tile_of([inner(targets, targets), inner(targets, image)])
-    gathered = gather(jnp.concatenate([image, sums], axis=0), "row", rows)
-    partial = image_terms(left, gathered[:, :NRHS], right)
-    sums = jnp.sum(gathered[:, NRHS:], axis=0)
-    partial = jnp.concatenate([partial, jnp.broadcast_to(sums[None], (cols,) + sums.shape)], axis=1)
+    partial = second_product(left, gather(image, "row", rows), high, low)
     reduced = jnp.sum(exchange(partial, "col"), axis=0)
     image_image = reduced[:NRHS] + noise * image
 
-    norm_now, curvature = reduced[NRHS, :NRHS], reduced[NRHS + 1, :NRHS]
+    norm_now, curvature = reduced[NRHS, :NRHS], reduced[NRHS, NRHS : 2 * NRHS]
     step_size = (norm_now / curvature)[:, None]
     residual = targets - step_size * image
     residual_image = image - step_size * image_image

time: 144 us -> 153 us (1.062)
  local copies, waits for them, and re-layouts: 1.38 us -> 23.8 us
  waiting for transfers between devices: 7.79 us -> 0.01 us
  Pallas kernels: 25.7 us -> 18.1 us
  blocking collectives: 92.8 us -> 95.6 us
  starting transfers between devices: 12.8 us -> 10.5 us
    all_gather x0 -> x1, blocking collectives: none -> 24.1 us  [on_device(): right = lax.all_gather(scaled, 'col', axis=0)]
    unnamed x4 -> x12, local copies, waits for them, and re-layouts: 0.64 us -> 23 us
    all_to_all x6 -> x5, blocking collectives: 92.8 us -> 71.5 us  [exchange(): return lax.all_to_all(blocks, axis, 0, 0, tiled=True)]
    all_to_all x1, waiting for transfers between devices: 7.79 us -> 0.01 us  [exchange(): return lax.all_to_all(blocks, axis, 0, 0, tiled=True)]
    pallas_call x2, Pallas kernels: 25.7 us -> 18.1 us  [the longest x1 12.8 us: first_product(): pl.pallas_call(first_kernel, out_shape=[jax.ShapeDtypeStruct((right.shape...]
    all_to_all x1, starting transfers between devices: 12.8 us -> 10.5 us  [exchange(): return lax.all_to_all(blocks, axis, 0, 0, tiled=True)]
  transfers between devices with their start and end apart: 1 -> 1, of which waited for: 1 -> 0; matrix products, arithmetic and copies ran while one was open for 0% -> 0% of each run, Pallas kernels for 0% -> 0%
where the time goes in v3:
time: 153 us; the launch traced here: 152 us
  blocking collectives  95.6 us (62%)
  local copies, waits for them, and re-layouts  23.8 us (16%)
  Pallas kernels  18.1 us (12%)
  starting transfers between devices  10.5 us (7%)
  other arithmetic  3.4 us (2%)
    all_to_all x5, blocking collectives, exchange(): return lax.all_to_all(blocks, axis, 0, 0, tiled=True)  71.5 us
    all_gather x1, blocking collectives, on_device(): right = lax.all_gather(scaled, 'col', axis=0)  24.1 us
    unnamed x12, local copies, waits for them, and re-layouts  23 us
    pallas_call x1, Pallas kernels, first_product(): pl.pallas_call(first_kernel, out_shape=[jax.ShapeDtypeStruct((right.shape...  12.8 us
    all_to_all x1, starting transfers between devices, exchange(): return lax.all_to_all(blocks, axis, 0, 0, tiled=True)  10.5 us
    pallas_call x1, Pallas kernels, second_product(): pl.pallas_call(second_kernel, out_shape=jax.ShapeDtypeStruct((right_count...  5.37 us
  transfers between devices with their start and end apart: 1, of which 0 were waited for; matrix products, arithmetic and copies ran while one was open for 0% of the time, Pallas kernels for 0%

profile of v3, /device:TPU:1, one launch (start us, length us, event | category | flops | bytes accessed | tf_op | source)
XLA Modules:
  0.0 152.1 jit_solution(14238765480535942367)
XLA Ops:
  0.6 0.8 broadcast_multiply_fusion
  1.4 0.7 pad_maximum_fusion
  2.1 0.8 broadcast_in_dim.8
  2.9 10.5 %all-to-all-start = ((f32[32,24,128]{2,1,0:T(8,128)}), f32[32,24,128]{2,1,0:T(8,128)S(1)}, u32[]{:S(2)}, u32[]{:S(2)}) async-start(f32[32,24,128]{2,1,0:T(8,128)} %broadcast_in_dim.8), calls=%async_computation | async-start | bytes 786432 | tf_op jit(solution)/shard_map/all_to_all | solution.py:146
  13.4 24.1 %all-gather = f32[128,128]{1,0:T(8,128)S(1)} all-gather(f32[8,128]{1,0:T(8,128)S(1)} %broadcast_multiply_fusion), channel_id=2, replica_groups=mesh['row'=32,'col'=16] {'col'}, dimensions={0}, use_global_device_ids=true | all-gather | bytes 69632 | tf_op jit(solution)/shard_map/all_gather | solution.py:166
  37.5 0.0 all-to-all-done.left_ref
  37.5 12.8 %shard_map.59 = (f32[16,16,128]{2,1,0:T(8,128)S(1)}, bf16[4096,2048]{1,0:T(8,128)(2,1)S(1)}, bf16[4096,2048]{1,0:T(8,128)(2,1)S(1)}) custom-call(f32[32,24,128]{2,1,0:T(8,128)S(1)} %all-to-all-done.left_ref, f32[16,8,128]{2,1,0:T(8,128)S(1)} %bitcast.31), custom_call_target="tpu_custom_call" | custom-call | tf_op jit(solution)/shard_map/pallas_call | solution.py:115
  50.3 0.0 copy-start
  50.3 5.7 %copy-done = bf16[4096,2048]{1,0:T(8,128)(2,1)} copy-done((bf16[4096,2048]{1,0:T(8,128)(2,1)}, bf16[4096,2048]{1,0:T(8,128)(2,1)S(1)}, u32[]{:S(2)}) %copy-start) | copy-done | bytes 16777240
  56.0 5.7 %copy-done.2 = bf16[4096,2048]{1,0:T(8,128)(2,1)} copy-done((bf16[4096,2048]{1,0:T(8,128)(2,1)}, bf16[4096,2048]{1,0:T(8,128)(2,1)S(1)}, u32[]{:S(2)}) %copy-start.2) | copy-done | bytes 16777240
  61.7 11.9 %all_to_all.30 = f32[16,16,128]{2,1,0:T(8,128)S(1)} all-to-all(f32[16,16,128]{2,1,0:T(8,128)S(1)} %get-tuple-element.5), channel_id=1, replica_groups=mesh['row'=32,'col'=16] {'col'}, dimensions={0} | all-to-all | bytes 262144 | tf_op jit(solution)/shard_map/all_to_all | solution.py:146
  73.6 0.8 multiply_add_fusion.1
  74.4 21.6 %all_to_all.31.image_ref = f32[32,16,128]{2,1,0:T(8,128)S(1)} all-to-all(f32[32,16,128]{2,1,0:T(8,128)S(1)} %broadcast_in_dim.9), channel_id=1, replica_groups=mesh['row'=32,'col'=16] {'row'}, dimensions={0} | all-to-all | bytes 524288 | tf_op jit(solution)/shard_map/all_to_all | solution.py:146
  96.0 5.8 %copy-done.1 = bf16[4096,2048]{1,0:T(8,128)(2,1)S(1)} copy-done((bf16[4096,2048]{1,0:T(8,128)(2,1)S(1)}, bf16[4096,2048]{1,0:T(8,128)(2,1)}, u32[]{:S(2)}) %copy-start.1) | copy-done | bytes 16777240
  101.7 5.8 %copy-done.3 = bf16[4096,2048]{1,0:T(8,128)(2,1)S(1)} copy-done((bf16[4096,2048]{1,0:T(8,128)(2,1)S(1)}, bf16[4096,2048]{1,0:T(8,128)(2,1)}, u32[]{:S(2)}) %copy-start.3) | copy-done | bytes 16777240
  107.5 5.4 %shard_map.60 = f32[16,24,128]{2,1,0:T(8,128)S(1)} custom-call(f32[32,24,128]{2,1,0:T(8,128)S(1)} %all-to-all-done.left_ref, f32[32,16,128]{2,1,0:T(8,128)S(1)} %all_to_all.31.image_ref, bf16[4096,2048]{1,0:T(8,128)(2,1)S(1)} %copy-done.1, bf16[4096,2048]{1,0:T(8,128)(2,1)S(1)} %copy-done.3), custom_call_target="tpu_custom_call" | custom-call | tf_op jit(solution)/shard_map/pallas_call | solution.py:132
  112.9 14.3 %all_to_all.32 = f32[16,24,128]{2,1,0:T(8,128)S(1)} all-to-all(f32[16,24,128]{2,1,0:T(8,128)S(1)} %shard_map.60), channel_id=1, replica_groups=mesh['row'=32,'col'=16] {'col'}, dimensions={0} | all-to-all | bytes 393216 | tf_op jit(solution)/shard_map/all_to_all | solution.py:146
  127.2 0.1 fusion.5
  127.3 0.0 copy-done.4
  127.3 0.2 multiply_reduce_fusion.2
  127.6 10.5 %all_to_all.33 = f32[16,8,128]{2,1,0:T(8,128)S(1)} all-to-all(f32[16,8,128]{2,1,0:T(8,128)S(1)} %broadcast_in_dim.10), channel_id=1, replica_groups=mesh['row'=32,'col'=16] {'col'}, dimensions={0} | all-to-all | bytes 131072 | tf_op jit(solution)/shard_map/all_to_all | solution.py:146
  138.1 13.3 %all_to_all.34 = f32[32,8,128]{2,1,0:T(8,128)S(1)} all-to-all(f32[32,8,128]{2,1,0:T(8,128)S(1)} %broadcast_in_dim.11), channel_id=1, replica_groups=mesh['row'=32,'col'=16] {'row'}, dimensions={0} | all-to-all | bytes 262144 | tf_op jit(solution)/shard_map/all_to_all | solution.py:146
  151.3 0.1 fusion.4
  151.4 0.7 multiply_subtract_fusion
  (14 shorter events, 0.2 us)
Async XLA Ops:
  2.9 34.6 %all-to-all-start = ((f32[32,24,128]{2,1,0:T(8,128)}), f32[32,24,128]{2,1,0:T(8,128)S(1)}, u32[]{:S(2)}, u32[]{:S(2)}) async-start(f32[32,24,128]{2,1,0:T(8,128)} %broadcast_in_dim.8), calls=%async_computation | async-start | bytes 786432 | tf_op jit(solution)/shard_map/all_to_all | solution.py:146
  50.3 5.7 %copy-start = (bf16[4096,2048]{1,0:T(8,128)(2,1)}, bf16[4096,2048]{1,0:T(8,128)(2,1)S(1)}, u32[]{:S(2)}) copy-start(bf16[4096,2048]{1,0:T(8,128)(2,1)S(1)} %get-tuple-element.6.high_ref) | copy-start | bytes 50331652
  56.0 5.7 %copy-start.2 = (bf16[4096,2048]{1,0:T(8,128)(2,1)}, bf16[4096,2048]{1,0:T(8,128)(2,1)S(1)}, u32[]{:S(2)}) copy-start(bf16[4096,2048]{1,0:T(8,128)(2,1)S(1)} %get-tuple-element.7.low_ref) | copy-start | bytes 50331652
  96.0 5.8 %copy-start.1 = (bf16[4096,2048]{1,0:T(8,128)(2,1)S(1)}, bf16[4096,2048]{1,0:T(8,128)(2,1)}, u32[]{:S(2)}) copy-start(bf16[4096,2048]{1,0:T(8,128)(2,1)} %copy-done) | copy-start | bytes 50331652
  101.7 5.8 %copy-start.3 = (bf16[4096,2048]{1,0:T(8,128)(2,1)S(1)}, bf16[4096,2048]{1,0:T(8,128)(2,1)}, u32[]{:S(2)}) copy-start(bf16[4096,2048]{1,0:T(8,128)(2,1)} %copy-done.2) | copy-start | bytes 50331652
  107.5 19.8 %copy-start.4 = (f32[16,128]{1,0:T(8,128)S(1)}, f32[16,128]{1,0:T(8,128)}, u32[]{:S(2)}) copy-start(f32[16,128]{1,0:T(8,128)} %param.6) | copy-start | bytes 24580
  107.5 19.8 %copy-start.5 = (f32[16]{0:T(128)S(1)}, f32[16]{0:T(128)}, u32[]{:S(2)}) copy-start(f32[16]{0:T(128)} %param.7) | copy-start | bytes 196

commit v4 on v3

--- a/solution.py
+++ b/solution.py
@@ -14,9 +14,11 @@
 SUMS = 8
 FEATURE_ROWS = 64
 ROOT_LOG2E = math.sqrt(math.log2(math.e))
-STEP = 512
+STEP = 1024
 WIDE = 256
-VMEM_LIMIT = 16 << 20
+KEPT = 3
+VMEM_LIMIT = 40 << 20
+SMALL_LIMIT = 4 << 20
 
 
 def pieces(value):
@@ -50,7 +52,19 @@
 def split_vector(value_of, vector):
     for block in range(vector.shape[1] // LANES):
         span = pl.ds(block * LANES, LANES)
-        vector[:, span] = jnp.concatenate(pieces(value_of(block)), axis=0).astype(jnp.bfloat16)
+        vector[:, span] = jnp.concatenate(pieces(value_of(block))[:2], axis=0).astype(jnp.bfloat16)
+
+
+def write_right(right_ref, right):
+    for block in range(right_ref.shape[0]):
+        span = pl.ds(block * LANES, LANES)
+        right[:, span] = features(right_ref[block], False).astype(jnp.bfloat16)
+
+
+def write_left(left_ref, left, begin):
+    for block in range(begin, left_ref.shape[0]):
+        span = pl.ds((block - begin) * LANES, LANES)
+        left[span, :] = features(left_ref[block, :NFEAT, :], True).T.astype(jnp.bfloat16)
 
 
 def write_terms(total, out_ref):
@@ -59,39 +73,98 @@
         out_ref[block, :NRHS, :] = terms[:NRHS] + terms[NRHS : 2 * NRHS] + terms[2 * NRHS :]
 
 
-def first_kernel(left_ref, right_ref, out_ref, high_ref, low_ref, left, right, vector, total):
-    for block in range(right_ref.shape[0]):
-        span = pl.ds(block * LANES, LANES)
-        right[:, span] = features(right_ref[block], False).astype(jnp.bfloat16)
-    for block in range(left_ref.shape[0]):
-        span = pl.ds(block * LANES, LANES)
-        left[span, :] = features(left_ref[block, :NFEAT, :], True).T.astype(jnp.bfloat16)
+def spans(total):
+    return [pl.ds(place * WIDE, WIDE) for place in range(total.shape[1] // WIDE)]
+
+
+def add_terms(total, span, vector_block, high, low):
+    total[: 2 * NRHS, span] += dot(vector_block, high)
+    total[2 * NRHS :, span] += dot(vector_block[:NRHS], low)
+
+
+def parts_of(left_block, right_block):
+    kernel = jnp.exp2(dot(left_block, right_block))
+    high = kernel.astype(jnp.bfloat16)
+    return high, (kernel - high.astype(jnp.float32)).astype(jnp.bfloat16)
+
+
+def rows_of(step):
+    return pl.ds(pl.multiple_of(step * STEP, STEP), STEP)
+
+
+def first_kernel(
+    left_ref, right_ref, out_ref, high_ref, low_ref, left, right, vector, total, high_part, low_part, sent
+):
+    steps, kept = left.shape[0] // STEP, high_part.shape[0] // STEP
+    write_right(right_ref, right)
+    write_left(left_ref, left, 0)
     split_vector(lambda block: left_ref[block, NFEAT:, :], vector)
     total[...] = jnp.zeros_like(total)
 
-    def advance(step, unused):
-        rows = pl.ds(pl.multiple_of(step * STEP, STEP), STEP)
-        left_block = left[rows, :]
-        vector_block = vector[:, rows]
-        for place in range(right.shape[1] // WIDE):
-            span = pl.ds(place * WIDE, WIDE)
-            kernel = jnp.exp2(dot(left_block, right[:, span]))
-            high = kernel.astype(jnp.bfloat16)
-            low = (kernel - high.astype(jnp.float32)).astype(jnp.bfloat16)
-            high_ref[rows, span] = high
-            low_ref[rows, span] = low
-            total[:, span] += dot(vector_block, high) + dot(vector_block, low)
+    def copies(step):
+        rows = rows_of(step)
+        return [
+            pltpu.make_async_copy(part.at[rows], ref.at[rows], sent.at[place, step])
+            for place, (part, ref) in enumerate([(high_part, high_ref), (low_part, low_ref)])
+        ]
+
+    def advance(step, unused, keep):
+        rows = rows_of(step)
+        for span in spans(total):
+            high, low = parts_of(left[rows, :], right[:, span])
+            if keep:
+                high_part[rows, span] = high
+                low_part[rows, span] = low
+            add_terms(total, span, vector[:, rows], high, low)
+        if keep:
+            for copy in copies(step):
+                copy.start()
         return unused
 
-    lax.fori_loop(0, left.shape[0] // STEP, advance, 0)
+    lax.fori_loop(0, kept, functools.partial(advance, keep=True), 0)
+    lax.fori_loop(kept, steps, functools.partial(advance, keep=False), 0)
     write_terms(total, out_ref)
-
-
-def second_kernel(left_ref, image_ref, high_ref, low_ref, out_ref, vector, total):
+    for step in range(kept):
+        for copy in copies(step):
+            copy.wait()
+
+
+def second_kernel(
+    left_ref, right_ref, image_ref, high_ref, low_ref, out_ref, left, right, vector, total, high_part, low_part, come
+):
+    steps, kept = vector.shape[1] // STEP, high_part.shape[0] // STEP
+
+    def copies(step):
+        rows = rows_of(step)
+        return [
+            pltpu.make_async_copy(ref.at[rows], part.at[rows], come.at[place, step])
+            for place, (part, ref) in enumerate([(high_part, high_ref), (low_part, low_ref)])
+        ]
+
+    for step in range(kept):
+        for copy in copies(step):
+            copy.start()
+    write_right(right_ref, right)
+    write_left(left_ref, left, kept * STEP // LANES)
     split_vector(lambda block: image_ref[block], vector)
-    for place in range(total.shape[1] // WIDE):
-        span = pl.ds(place * WIDE, WIDE)
-        total[:, span] = dot(vector[...], high_ref[:, span]) + dot(vector[...], low_ref[:, span])
+    total[...] = jnp.zeros_like(total)
+
+    def compute(step, unused):
+        for span in spans(total):
+            high, low = parts_of(left[rows_of(step - kept), :], right[:, span])
+            add_terms(total, span, vector[:, rows_of(step)], high, low)
+        return unused
+
+    def multiply(step, unused):
+        rows = rows_of(step)
+        for copy in copies(step):
+            copy.wait()
+        for span in spans(total):
+            add_terms(total, span, vector[:, rows], high_part[rows, span], low_part[rows, span])
+        return unused
+
+    lax.fori_loop(kept, steps, compute, 0)
+    lax.fori_loop(0, kept, multiply, 0)
     write_terms(total, out_ref)
     square = jnp.zeros((NRHS, LANES), jnp.float32)
     product = jnp.zeros((NRHS, LANES), jnp.float32)
@@ -106,40 +179,96 @@
         out_ref[block, NRHS:, :] = jnp.broadcast_to(row, (SUMS, LANES))
 
 
+def known_kernel(scale_ref, points_ref, targets_ref, scaled_ref, spread_ref):
+    for feature in range(NFEAT):
+        row = slice(feature, feature + 1)
+        scaled_ref[row, :] = points_ref[row, :] * scale_ref[feature]
+    for block in range(spread_ref.shape[0]):
+        spread_ref[block, :NFEAT, :] = scaled_ref[...]
+        spread_ref[block, NFEAT:, :] = targets_ref[...]
+
+
+def image_kernel(noise_ref, targets_ref, terms_ref, image_ref, spread_ref):
+    for place in range(NRHS):
+        row = slice(place, place + 1)
+        image_ref[row, :] = targets_ref[row, :] * noise_ref[place]
+    image = image_ref[...]
+    for block in range(terms_ref.shape[0]):
+        image += terms_ref[block]
+    image_ref[...] = image
+    for block in range(spread_ref.shape[0]):
+        spread_ref[block] = image
+
+
 VMEM_BLOCK = pl.BlockSpec(memory_space=pltpu.VMEM)
+
+
+ANY_BLOCK = pl.BlockSpec(memory_space=pl.ANY)
+SMEM_BLOCK = pl.BlockSpec(memory_space=pltpu.SMEM)
+
+
+def spread_known(inverse_scale, points, targets, count):
+    return pl.pallas_call(
+        known_kernel,
+        out_shape=[
+            jax.ShapeDtypeStruct(points.shape, jnp.float32),
+            jax.ShapeDtypeStruct((count, NFEAT + NRHS, LANES), jnp.float32),
+        ],
+        in_specs=[SMEM_BLOCK, VMEM_BLOCK, VMEM_BLOCK],
+        out_specs=[VMEM_BLOCK] * 2,
+        compiler_params=pltpu.CompilerParams(vmem_limit_bytes=SMALL_LIMIT),
+    )(inverse_scale, points, targets)
+
+
+def spread_image(noise_var, targets, terms, count):
+    return pl.pallas_call(
+        image_kernel,
+        out_shape=[
+            jax.ShapeDtypeStruct(targets.shape, jnp.float32),
+            jax.ShapeDtypeStruct((count,) + targets.shape, jnp.float32),
+        ],
+        in_specs=[SMEM_BLOCK, VMEM_BLOCK, VMEM_BLOCK],
+        out_specs=[VMEM_BLOCK] * 2,
+        compiler_params=pltpu.CompilerParams(vmem_limit_bytes=SMALL_LIMIT),
+    )(noise_var, targets, terms)
+
+
+def scratch(left_count, feature_count, right_count):
+    part = pltpu.VMEM((KEPT * STEP, right_count), jnp.bfloat16)
+    return [
+        pltpu.VMEM((feature_count, FEATURE_ROWS), jnp.bfloat16),
+        pltpu.VMEM((FEATURE_ROWS, right_count), jnp.bfloat16),
+        pltpu.VMEM((2 * NRHS, left_count), jnp.bfloat16),
+        pltpu.VMEM((3 * NRHS, right_count), jnp.float32),
+        part,
+        part,
+        pltpu.SemaphoreType.DMA((2, KEPT)),
+    ]
 
 
 def first_product(left, right):
     left_count, right_count = left.shape[0] * LANES, right.shape[0] * LANES
-    kept = pltpu.VMEM((left_count, right_count), jnp.bfloat16)
+    part = jax.ShapeDtypeStruct((KEPT * STEP, right_count), jnp.bfloat16)
     return pl.pallas_call(
         first_kernel,
-        out_shape=[jax.ShapeDtypeStruct((right.shape[0], NRHS, LANES), jnp.float32), kept, kept],
+        out_shape=[jax.ShapeDtypeStruct((right.shape[0], NRHS, LANES), jnp.float32), part, part],
         in_specs=[VMEM_BLOCK] * 2,
-        out_specs=[VMEM_BLOCK] * 3,
-        scratch_shapes=[
-            pltpu.VMEM((left_count, FEATURE_ROWS), jnp.bfloat16),
-            pltpu.VMEM((FEATURE_ROWS, right_count), jnp.bfloat16),
-            pltpu.VMEM((3 * NRHS, left_count), jnp.bfloat16),
-            pltpu.VMEM((3 * NRHS, right_count), jnp.float32),
-        ],
+        out_specs=[VMEM_BLOCK, ANY_BLOCK, ANY_BLOCK],
+        scratch_shapes=scratch(left_count, left_count, right_count),
         compiler_params=pltpu.CompilerParams(vmem_limit_bytes=VMEM_LIMIT),
     )(left, right)
 
 
-def second_product(left, image, high, low):
-    left_count, right_count = high.shape
+def second_product(left, right, image, high, low):
+    left_count, right_count = left.shape[0] * LANES, right.shape[0] * LANES
     return pl.pallas_call(
         second_kernel,
-        out_shape=jax.ShapeDtypeStruct((right_count // LANES, NRHS + SUMS, LANES), jnp.float32),
-        in_specs=[VMEM_BLOCK] * 4,
+        out_shape=jax.ShapeDtypeStruct((right.shape[0], NRHS + SUMS, LANES), jnp.float32),
+        in_specs=[VMEM_BLOCK] * 3 + [ANY_BLOCK] * 2,
         out_specs=VMEM_BLOCK,
-        scratch_shapes=[
-            pltpu.VMEM((3 * NRHS, left_count), jnp.bfloat16),
-            pltpu.VMEM((3 * NRHS, right_count), jnp.float32),
-        ],
+        scratch_shapes=scratch(left_count, left_count - KEPT * STEP, right_count),
         compiler_params=pltpu.CompilerParams(vmem_limit_bytes=VMEM_LIMIT),
-    )(left, image, high, low)
+    )(left, right, image, high, low)
 
 
 def exchange(blocks, axis):
@@ -160,14 +289,14 @@
 
 
 def on_device(rows, cols, points, inverse_scale, targets, noise_var):
+    scaled, spread = spread_known(inverse_scale, points, targets, rows)
+    left = exchange(spread, "row")
+    right = lax.all_gather(scaled, "col", axis=0)
+
+    partial, high, low = first_product(left, right)
+    image, spread = spread_image(noise_var, targets, exchange(partial, "col"), rows)
+    partial = second_product(left, right, exchange(spread, "row"), high, low)
     noise = noise_var[:, None]
-    scaled = points * inverse_scale[:, None]
-    left = gather(jnp.concatenate([scaled, targets], axis=0), "row", rows)
-    right = lax.all_gather(scaled, "col", axis=0)
-
-    partial, high, low = first_product(left, right)
-    image = jnp.sum(exchange(partial, "col"), axis=0) + noise * targets
-    partial = second_product(left, gather(image, "row", rows), high, low)
     reduced = jnp.sum(exchange(partial, "col"), axis=0)
     image_image = reduced[:NRHS] + noise * image
 

time: 153 us -> 142 us (0.928)
  local copies, waits for them, and re-layouts: 23.8 us -> 12.5 us
  Pallas kernels: 18.1 us -> 21 us
  other arithmetic: 3.4 us -> 1.15 us
    unnamed x12 -> x18, local copies, waits for them, and re-layouts: 23 us -> 12.4 us
    pallas_call x1 -> x3, Pallas kernels: 5.37 us -> 9.3 us  [the longest x1 7.41 us: second_product(): pl.pallas_call(second_kernel, out_shape=jax.ShapeDtypeStruct((right.shape...]
where the time goes in v4:
time: 142 us; the launch traced here: 141 us
  blocking collectives  95.6 us (67%)
  Pallas kernels  21 us (15%)
  local copies, waits for them, and re-layouts  12.5 us (9%)
  starting transfers between devices  10.5 us (7%)
    all_to_all x5, blocking collectives, exchange(): return lax.all_to_all(blocks, axis, 0, 0, tiled=True)  71.5 us
    all_gather x1, blocking collectives, on_device(): right = lax.all_gather(scaled, 'col', axis=0)  24.1 us
    unnamed x18, local copies, waits for them, and re-layouts  12.4 us
    pallas_call x1, Pallas kernels, first_product(): pl.pallas_call(first_kernel, out_shape=[jax.ShapeDtypeStruct((right.shape...  11.7 us
    all_to_all x1, starting transfers between devices, exchange(): return lax.all_to_all(blocks, axis, 0, 0, tiled=True)  10.5 us
    pallas_call x1, Pallas kernels, second_product(): pl.pallas_call(second_kernel, out_shape=jax.ShapeDtypeStruct((right.shape...  7.41 us
  transfers between devices with their start and end apart: 1, of which 0 were waited for; matrix products, arithmetic and copies ran while one was open for 0% of the time, Pallas kernels for 0%

profile of v4, /device:TPU:1, one launch (start us, length us, event | category | flops | bytes accessed | tf_op | source)
XLA Modules:
  0.0 141.4 jit_solution(4815583090175839261)
XLA Ops:
  0.6 0.0 copy-start.2
  0.6 0.7 copy-done.2
  1.3 0.7 copy-done.7
  2.0 0.7 copy-done.8
  2.7 1.3 shard_map.59
  4.0 10.5 %all-to-all-start = ((f32[32,24,128]{2,1,0:T(8,128)}), f32[32,24,128]{2,1,0:T(8,128)S(1)}, u32[]{:S(2)}, u32[]{:S(2)}) async-start(f32[32,24,128]{2,1,0:T(8,128)} %get-tuple-element.9), calls=%async_computation | async-start | bytes 786432 | tf_op jit(solution)/shard_map/all_to_all | solution.py:275
  14.5 24.1 %all-gather = f32[128,128]{1,0:T(8,128)S(1)} all-gather(f32[8,128]{1,0:T(8,128)S(1)} %get-tuple-element.10), channel_id=2, replica_groups=mesh['row'=32,'col'=16] {'col'}, dimensions={0}, use_global_device_ids=true | all-gather | bytes 69632 | tf_op jit(solution)/shard_map/all_gather | solution.py:294
  38.6 0.0 all-to-all-done.left_ref
  38.6 11.7 %shard_map.60 = (f32[16,16,128]{2,1,0:T(8,128)S(1)}, bf16[3072,2048]{1,0:T(8,128)(2,1)S(1)}, bf16[3072,2048]{1,0:T(8,128)(2,1)}) custom-call(f32[32,24,128]{2,1,0:T(8,128)S(1)} %all-to-all-done.left_ref, f32[16,8,128]{2,1,0:T(8,128)S(1)} %bitcast.31), custom_call_target="tpu_custom_call" | custom-call | tf_op jit(solution)/shard_map/pallas_call | solution.py:252
  50.3 4.5 %copy-done = bf16[3072,2048]{1,0:T(8,128)(2,1)} copy-done((bf16[3072,2048]{1,0:T(8,128)(2,1)}, bf16[3072,2048]{1,0:T(8,128)(2,1)S(1)}, u32[]{:S(2)}) %copy-start) | copy-done | bytes 12582936
  54.8 11.8 %all_to_all.30.terms_ref = f32[16,16,128]{2,1,0:T(8,128)S(1)} all-to-all(f32[16,16,128]{2,1,0:T(8,128)S(1)} %get-tuple-element.11), channel_id=1, replica_groups=mesh['row'=32,'col'=16] {'col'}, dimensions={0} | all-to-all | bytes 262144 | tf_op jit(solution)/shard_map/all_to_all | solution.py:275
  66.6 0.7 copy-done.3
  67.3 0.7 copy-done.5
  68.0 0.6 shard_map.61
  68.6 21.6 %all_to_all.31.image_ref = f32[32,16,128]{2,1,0:T(8,128)S(1)} all-to-all(f32[32,16,128]{2,1,0:T(8,128)S(1)} %get-tuple-element.12), channel_id=1, replica_groups=mesh['row'=32,'col'=16] {'row'}, dimensions={0} | all-to-all | bytes 524288 | tf_op jit(solution)/shard_map/all_to_all | solution.py:275
  90.1 4.6 %copy-done.1 = bf16[3072,2048]{1,0:T(8,128)(2,1)S(1)} copy-done((bf16[3072,2048]{1,0:T(8,128)(2,1)S(1)}, bf16[3072,2048]{1,0:T(8,128)(2,1)}, u32[]{:S(2)}) %copy-start.1) | copy-done | bytes 12582936
  94.7 7.4 %shard_map.62 = f32[16,24,128]{2,1,0:T(8,128)S(1)} custom-call(f32[32,24,128]{2,1,0:T(8,128)S(1)} %all-to-all-done.left_ref, f32[16,8,128]{2,1,0:T(8,128)S(1)} %bitcast.32, f32[32,16,128]{2,1,0:T(8,128)S(1)} %all_to_all.31.image_ref, bf16[3072,2048]{1,0:T(8,128)(2,1)S(1)} %copy-done.1, bf16[3072,2048]{1,0:T(8,128)(2,1)} %get-tuple-element.14.low_ref), custom_call_target="tpu_custom_call" | custom-call | tf_op jit(solution)/shard_map/pallas_call | solution.py:264
  102.1 14.4 %all_to_all.32 = f32[16,24,128]{2,1,0:T(8,128)S(1)} all-to-all(f32[16,24,128]{2,1,0:T(8,128)S(1)} %shard_map.62), channel_id=1, replica_groups=mesh['row'=32,'col'=16] {'col'}, dimensions={0} | all-to-all | bytes 393216 | tf_op jit(solution)/shard_map/all_to_all | solution.py:275
  116.5 0.1 fusion.5
  116.6 0.2 multiply_reduce_fusion.2
  116.8 10.5 %all_to_all.33 = f32[16,8,128]{2,1,0:T(8,128)S(1)} all-to-all(f32[16,8,128]{2,1,0:T(8,128)S(1)} %broadcast_in_dim.4), channel_id=1, replica_groups=mesh['row'=32,'col'=16] {'col'}, dimensions={0} | all-to-all | bytes 131072 | tf_op jit(solution)/shard_map/all_to_all | solution.py:275
  127.3 13.2 %all_to_all.34 = f32[32,8,128]{2,1,0:T(8,128)S(1)} all-to-all(f32[32,8,128]{2,1,0:T(8,128)S(1)} %broadcast_in_dim.5), channel_id=1, replica_groups=mesh['row'=32,'col'=16] {'row'}, dimensions={0} | all-to-all | bytes 262144 | tf_op jit(solution)/shard_map/all_to_all | solution.py:275
  140.6 0.1 fusion.4
  140.7 0.7 multiply_subtract_fusion
  (16 shorter events, 0.1 us)
Async XLA Ops:
  0.6 0.7 copy-start.2
  1.3 0.7 copy-start.7
  2.0 0.7 copy-start.8
  4.0 34.6 %all-to-all-start = ((f32[32,24,128]{2,1,0:T(8,128)}), f32[32,24,128]{2,1,0:T(8,128)S(1)}, u32[]{:S(2)}, u32[]{:S(2)}) async-start(f32[32,24,128]{2,1,0:T(8,128)} %get-tuple-element.9), calls=%async_computation | async-start | bytes 786432 | tf_op jit(solution)/shard_map/all_to_all | solution.py:275
  50.3 4.5 %copy-start = (bf16[3072,2048]{1,0:T(8,128)(2,1)}, bf16[3072,2048]{1,0:T(8,128)(2,1)S(1)}, u32[]{:S(2)}) copy-start(bf16[3072,2048]{1,0:T(8,128)(2,1)S(1)} %get-tuple-element.13.high_ref) | copy-start | bytes 37748740
  66.6 0.7 copy-start.3
  67.3 0.7 copy-start.5
  90.1 4.6 %copy-start.1 = (bf16[3072,2048]{1,0:T(8,128)(2,1)S(1)}, bf16[3072,2048]{1,0:T(8,128)(2,1)}, u32[]{:S(2)}) copy-start(bf16[3072,2048]{1,0:T(8,128)(2,1)} %copy-done) | copy-start | bytes 37748740
  94.7 21.9 %copy-start.4 = (f32[16,128]{1,0:T(8,128)S(1)}, f32[16,128]{1,0:T(8,128)}, u32[]{:S(2)}) copy-start(f32[16,128]{1,0:T(8,128)} %targets_ref.3) | copy-start | bytes 24580
  94.7 21.9 %copy-start.6 = (f32[16]{0:T(128)S(1)}, f32[16]{0:T(128)}, u32[]{:S(2)}) copy-start(f32[16]{0:T(128)} %noise_ref.1) | copy-start | bytes 196

commit v5 on v1

v5 whole, which is shorter than its diff:
```python
import functools
import math

import jax
import jax.numpy as jnp
from jax import lax
from jax.experimental import pallas as pl
from jax.experimental.pallas import tpu as pltpu
from jax.sharding import PartitionSpec as P

LANES = 128
NFEAT = 8
NRHS = 16
SUMS = 8
FEATURE_ROWS = 64
ROOT_LOG2E = math.sqrt(math.log2(math.e))
WIDE = 256
VMEM_LIMIT = 40 << 20


def pieces(value):
    high = value.astype(jnp.bfloat16).astype(jnp.float32)
    rest = value - high
    middle = rest.astype(jnp.bfloat16).astype(jnp.float32)
    low = (rest - middle).astype(jnp.bfloat16).astype(jnp.float32)
    return high, middle, low


def features(scaled, is_left):
    z = scaled * ROOT_LOG2E
    high, middle, low = pieces(z)
    norm_pieces = pieces(-0.5 * jnp.sum(z * z, axis=0, keepdims=True))
    row = lax.broadcasted_iota(jnp.int32, z.shape, 0)
    start = 0 if is_left else 3
    norms = jnp.where((row < 6) & ((row < start) | (row >= start + 3)), 1.0, 0.0)
    for place, piece in enumerate(norm_pieces):
        norms = jnp.where(row == start + place, piece, norms)
    if is_left:
        parts = [high, high, middle, middle, high, low]
    else:
        parts = [high, middle, high, middle, low, high]
    return jnp.concatenate(parts + [norms, jnp.zeros_like(z)], axis=0)


def dot(left, right):
    return lax.dot_general(left, right, (((1,), (0,)), ((), ())), preferred_element_type=jnp.float32)


def split_vector(value_of, vector):
    for block in range(vector.shape[1] // LANES):
        span = pl.ds(block * LANES, LANES)
        vector[:, span] = jnp.concatenate(pieces(value_of(block))[:2], axis=0).astype(jnp.bfloat16)


def write_right(right_ref, right):
    for block in range(right_ref.shape[0]):
        span = pl.ds(block * LANES, LANES)
        right[:, span] = features(right_ref[block], False).astype(jnp.bfloat16)


def write_left(left_ref, left):
    for block in range(left_ref.shape[0]):
        span = pl.ds(block * LANES, LANES)
        left[span, :] = features(left_ref[block, :NFEAT, :], True).T.astype(jnp.bfloat16)


def write_terms(total, out_ref):
    for block in range(out_ref.shape[0]):
        terms = total[:, pl.ds(block * LANES, LANES)]
        out_ref[block, :NRHS, :] = terms[:NRHS] + terms[NRHS : 2 * NRHS] + terms[2 * NRHS :]


def parts_of(left_block, right_block):
    kernel = jnp.exp2(dot(left_block, right_block))
    high = kernel.astype(jnp.bfloat16)
    return high, (kernel - high.astype(jnp.float32)).astype(jnp.bfloat16)


def write_total(vector, high, low, span, total):
    total[: 2 * NRHS, span] = dot(vector[...], high)
    total[2 * NRHS :, span] = dot(vector[:NRHS, :], low)


def multiply(left_ref, right_ref, value_of, out_ref, left, right, vector, total):
    write_right(right_ref, right)
    write_left(left_ref, left)
    split_vector(value_of, vector)
    for place in range(total.shape[1] // WIDE):
        span = pl.ds(place * WIDE, WIDE)
        high, low = parts_of(left[...], right[:, span])
        write_total(vector, high, low, span, total)
    write_terms(total, out_ref)


def first_kernel(left_ref, right_ref, out_ref, *scratch_refs):
    multiply(left_ref, right_ref, lambda block: left_ref[block, NFEAT:, :], out_ref, *scratch_refs)


def second_kernel(left_ref, right_ref, image_ref, out_ref, *scratch_refs):
    multiply(left_ref, right_ref, lambda block: image_ref[block], out_ref, *scratch_refs)
    square = jnp.zeros((NRHS, LANES), jnp.float32)
    product = jnp.zeros((NRHS, LANES), jnp.float32)
    for block in range(left_ref.shape[0]):
        target = left_ref[block, NFEAT:, :]
        square += target * target
        product += target * image_ref[block]
    empty = jnp.zeros((LANES - 2 * NRHS, LANES), jnp.float32)
    turned = jnp.concatenate([square, product, empty], axis=0).T
    row = jnp.sum(turned, axis=0, keepdims=True)
    for block in range(out_ref.shape[0]):
        out_ref[block, NRHS:, :] = jnp.broadcast_to(row, (SUMS, LANES))


VMEM_BLOCK = pl.BlockSpec(memory_space=pltpu.VMEM)


def image_terms(body, rows, left, right, *others):
    left_count, right_count = left.shape[0] * LANES, right.shape[0] * LANES
    return pl.pallas_call(
        body,
        out_shape=jax.ShapeDtypeStruct((right.shape[0], rows, LANES), jnp.float32),
        in_specs=[VMEM_BLOCK] * (2 + len(others)),
        out_specs=VMEM_BLOCK,
        scratch_shapes=[
            pltpu.VMEM((left_count, FEATURE_ROWS), jnp.bfloat16),
            pltpu.VMEM((FEATURE_ROWS, right_count), jnp.bfloat16),
            pltpu.VMEM((2 * NRHS, left_count), jnp.bfloat16),
            pltpu.VMEM((3 * NRHS, right_count), jnp.float32),
        ],
        compiler_params=pltpu.CompilerParams(vmem_limit_bytes=VMEM_LIMIT),
    )(left, right, *others)


def exchange(blocks, axis):
    return lax.all_to_all(blocks, axis, 0, 0, tiled=True)


def gather(block, axis, count):
    return exchange(jnp.broadcast_to(block[None], (count,) + block.shape), axis)


def tile_of(sums):
    stacked = jnp.stack(sums)
    return jnp.pad(stacked, ((0, SUMS - stacked.shape[0]), (0, LANES - NRHS)))


def inner(left, right):
    return jnp.sum(left * right, axis=1)


def on_device(rows, cols, points, inverse_scale, targets, noise_var):
    noise = noise_var[:, None]
    known = lax.optimization_barrier(jnp.concatenate([points * inverse_scale[:, None], targets], axis=0))
    targets = known[NFEAT:]
    left = gather(known, "row", rows)
    right = lax.all_gather(known[:NFEAT], "col", axis=0)

    partial = image_terms(first_kernel, NRHS, left, right)
    image = jnp.sum(exchange(partial, "col"), axis=0) + noise * targets
    partial = image_terms(second_kernel, NRHS + SUMS, left, right, gather(image, "row", rows))
    reduced = jnp.sum(exchange(partial, "col"), axis=0)
    image_image = reduced[:NRHS] + noise * image

    norm_now, curvature = reduced[NRHS, :NRHS], reduced[NRHS, NRHS : 2 * NRHS]
    step_size = (norm_now / curvature)[:, None]
    residual = targets - step_size * image
    residual_image = image - step_size * image_image
    sums = tile_of([inner(residual, residual), inner(residual, residual_image), inner(residual, image)])
    sums = jnp.sum(gather(sums, "col", cols), axis=0)
    sums = jnp.sum(gather(sums, "row", rows), axis=0)
    norm_next = sums[0, :NRHS]
    ratio = norm_next / norm_now
    next_curvature = sums[1, :NRHS] + ratio * (2.0 * sums[2, :NRHS] + ratio * curvature)
    next_step = (norm_next / next_curvature)[:, None]
    ratio = ratio[:, None]
    solution = step_size * targets + next_step * (residual + ratio * targets)
    residual = residual - next_step * (residual_image + ratio * image)
    return (solution, residual)


def solution(mesh):
    return jax.shard_map(
        functools.partial(on_device, mesh.shape["row"], mesh.shape["col"]),
        mesh=mesh,
        in_specs=(P(None, ("row", "col")), P(), P(None, ("row", "col")), P()),
        out_specs=(P(None, ("row", "col")), P(None, ("row", "col"))),
        check_vma=False,
    )
```

time: 144 us -> 130 us (0.903)
  waiting for transfers between devices: 7.79 us -> 0.01 us
  Pallas kernels: 25.7 us -> 19.4 us
  blocking collectives: 92.8 us -> 95.6 us
  starting transfers between devices: 12.8 us -> 10.5 us
    all_gather x0 -> x1, blocking collectives: none -> 24.1 us  [on_device(): right = lax.all_gather(known[:NFEAT], 'col', axis=0)]
    all_to_all x6 -> x5, blocking collectives: 92.8 us -> 71.5 us  [exchange(): return lax.all_to_all(blocks, axis, 0, 0, tiled=True)]
    all_to_all x1, waiting for transfers between devices: 7.79 us -> 0.01 us  [exchange(): return lax.all_to_all(blocks, axis, 0, 0, tiled=True)]
    pallas_call x2, Pallas kernels: 25.7 us -> 19.4 us  [image_terms(): pl.pallas_call(body, out_shape=jax.ShapeDtypeStruct((right.shape[0], rows...]
    all_to_all x1, starting transfers between devices: 12.8 us -> 10.5 us  [exchange(): return lax.all_to_all(blocks, axis, 0, 0, tiled=True)]
  transfers between devices with their start and end apart: 1 -> 1, of which waited for: 1 -> 0; matrix products, arithmetic and copies ran while one was open for 0% -> 0% of each run, Pallas kernels for 0% -> 0%
where the time goes in v5:
time: 130 us
  blocking collectives  95.6 us (74%)
  Pallas kernels  19.4 us (15%)
  starting transfers between devices  10.5 us (8%)
  other arithmetic  2.01 us (2%)
  local copies, waits for them, and re-layouts  1.45 us (1%)
    all_to_all x5, blocking collectives, exchange(): return lax.all_to_all(blocks, axis, 0, 0, tiled=True)  71.5 us
    all_gather x1, blocking collectives, on_device(): right = lax.all_gather(known[:NFEAT], 'col', axis=0)  24.1 us
    pallas_call x2, Pallas kernels, image_terms(): pl.pallas_call(body, out_shape=jax.ShapeDtypeStruct((right.shape[0], rows...  19.4 us
    all_to_all x1, starting transfers between devices, exchange(): return lax.all_to_all(blocks, axis, 0, 0, tiled=True)  10.5 us
  transfers between devices with their start and end apart: 1, of which 0 were waited for; matrix products, arithmetic and copies ran while one was open for 0% of the time, Pallas kernels for 0%

profile of v5, /device:TPU:1, one launch (start us, length us, event | category | flops | bytes accessed | tf_op | source)
XLA Modules:
  0.0 129.7 jit_solution(12567009227957167034)
XLA Ops:
  0.6 0.0 copy-start
  0.6 0.8 broadcast_multiply_fusion
  1.4 0.0 copy-done
  1.4 0.8 broadcast_in_dim.8
  2.2 10.5 %all-to-all-start = ((f32[32,24,128]{2,1,0:T(8,128)}), f32[32,24,128]{2,1,0:T(8,128)S(1)}, u32[]{:S(2)}, u32[]{:S(2)}) async-start(f32[32,24,128]{2,1,0:T(8,128)} %broadcast_in_dim.8), calls=%async_computation | async-start | bytes 786432 | tf_op jit(solution)/shard_map/all_to_all | solution.py:135
  12.7 24.1 %all-gather = f32[128,128]{1,0:T(8,128)S(1)} all-gather(f32[8,128]{1,0:T(8,128)S(1)} %slice.32), channel_id=2, replica_groups=mesh['row'=32,'col'=16] {'col'}, dimensions={0}, use_global_device_ids=true | all-gather | bytes 69632 | tf_op jit(solution)/shard_map/all_gather | solution.py:156
  36.8 0.0 all-to-all-done.left_ref
  36.8 9.7 %shard_map.59 = f32[16,16,128]{2,1,0:T(8,128)S(1)} custom-call(f32[32,24,128]{2,1,0:T(8,128)S(1)} %all-to-all-done.left_ref, f32[16,8,128]{2,1,0:T(8,128)S(1)} %bitcast.31), custom_call_target="tpu_custom_call" | custom-call | tf_op jit(solution)/shard_map/pallas_call | solution.py:119
  46.5 11.9 %all_to_all.30 = f32[16,16,128]{2,1,0:T(8,128)S(1)} all-to-all(f32[16,16,128]{2,1,0:T(8,128)S(1)} %shard_map.59), channel_id=1, replica_groups=mesh['row'=32,'col'=16] {'col'}, dimensions={0} | all-to-all | bytes 262144 | tf_op jit(solution)/shard_map/all_to_all | solution.py:135
  58.4 0.0 copy-start.1
  58.4 0.6 copy-done.1
  59.0 0.1 multiply_add_fusion.1
  59.1 21.6 %all_to_all.31.image_ref = f32[32,16,128]{2,1,0:T(8,128)S(1)} all-to-all(f32[32,16,128]{2,1,0:T(8,128)S(1)} %broadcast_in_dim.9), channel_id=1, replica_groups=mesh['row'=32,'col'=16] {'row'}, dimensions={0} | all-to-all | bytes 524288 | tf_op jit(solution)/shard_map/all_to_all | solution.py:135
  80.7 9.7 %shard_map.60 = f32[16,24,128]{2,1,0:T(8,128)S(1)} custom-call(f32[32,24,128]{2,1,0:T(8,128)S(1)} %all-to-all-done.left_ref, f32[16,8,128]{2,1,0:T(8,128)S(1)} %bitcast.32, f32[32,16,128]{2,1,0:T(8,128)S(1)} %all_to_all.31.image_ref), custom_call_target="tpu_custom_call" | custom-call | tf_op jit(solution)/shard_map/pallas_call | solution.py:119
  90.4 14.3 %all_to_all.32 = f32[16,24,128]{2,1,0:T(8,128)S(1)} all-to-all(f32[16,24,128]{2,1,0:T(8,128)S(1)} %shard_map.60), channel_id=1, replica_groups=mesh['row'=32,'col'=16] {'col'}, dimensions={0} | all-to-all | bytes 393216 | tf_op jit(solution)/shard_map/all_to_all | solution.py:135
  104.8 0.1 fusion.5
  104.9 0.2 multiply_reduce_fusion.2
  105.1 10.5 %all_to_all.33 = f32[16,8,128]{2,1,0:T(8,128)S(1)} all-to-all(f32[16,8,128]{2,1,0:T(8,128)S(1)} %broadcast_in_dim.10), channel_id=1, replica_groups=mesh['row'=32,'col'=16] {'col'}, dimensions={0} | all-to-all | bytes 131072 | tf_op jit(solution)/shard_map/all_to_all | solution.py:135
  115.6 13.2 %all_to_all.34 = f32[32,8,128]{2,1,0:T(8,128)S(1)} all-to-all(f32[32,8,128]{2,1,0:T(8,128)S(1)} %broadcast_in_dim.11), channel_id=1, replica_groups=mesh['row'=32,'col'=16] {'row'}, dimensions={0} | all-to-all | bytes 262144 | tf_op jit(solution)/shard_map/all_to_all | solution.py:135
  128.9 0.1 fusion.4
  129.0 0.7 multiply_subtract_fusion
  (10 shorter events, 0.2 us)
Async XLA Ops:
  0.6 0.8 copy-start
  2.2 34.6 %all-to-all-start = ((f32[32,24,128]{2,1,0:T(8,128)}), f32[32,24,128]{2,1,0:T(8,128)S(1)}, u32[]{:S(2)}, u32[]{:S(2)}) async-start(f32[32,24,128]{2,1,0:T(8,128)} %broadcast_in_dim.8), calls=%async_computation | async-start | bytes 786432 | tf_op jit(solution)/shard_map/all_to_all | solution.py:135
  58.4 0.7 copy-start.1

commit v6 on v5

--- a/solution.py
+++ b/solution.py
@@ -15,6 +15,7 @@
 FEATURE_ROWS = 64
 ROOT_LOG2E = math.sqrt(math.log2(math.e))
 WIDE = 256
+CHUNK = 512
 VMEM_LIMIT = 40 << 20
 
 
@@ -76,9 +77,9 @@
     return high, (kernel - high.astype(jnp.float32)).astype(jnp.bfloat16)
 
 
-def write_total(vector, high, low, span, total):
-    total[: 2 * NRHS, span] = dot(vector[...], high)
-    total[2 * NRHS :, span] = dot(vector[:NRHS, :], low)
+def chunk_terms(left, right, vector, rows, span):
+    high, low = parts_of(left[rows, :], right[:, span])
+    return jnp.concatenate([dot(vector[:, rows], high), dot(vector[:NRHS, rows], low)], axis=0)
 
 
 def multiply(left_ref, right_ref, value_of, out_ref, left, right, vector, total):
@@ -87,8 +88,8 @@
     split_vector(value_of, vector)
     for place in range(total.shape[1] // WIDE):
         span = pl.ds(place * WIDE, WIDE)
-        high, low = parts_of(left[...], right[:, span])
-        write_total(vector, high, low, span, total)
+        terms = [chunk_terms(left, right, vector, pl.ds(begin, CHUNK), span) for begin in range(0, left.shape[0], CHUNK)]
+        total[:, span] = functools.reduce(jnp.add, terms)
     write_terms(total, out_ref)
 
 
@@ -139,9 +140,8 @@
     return exchange(jnp.broadcast_to(block[None], (count,) + block.shape), axis)
 
 
-def tile_of(sums):
-    stacked = jnp.stack(sums)
-    return jnp.pad(stacked, ((0, SUMS - stacked.shape[0]), (0, LANES - NRHS)))
+def row_of(sums):
+    return jnp.pad(jnp.concatenate(sums), (0, LANES - NRHS * len(sums)))[None]
 
 
 def inner(left, right):
@@ -150,13 +150,14 @@
 
 def on_device(rows, cols, points, inverse_scale, targets, noise_var):
     noise = noise_var[:, None]
-    known = lax.optimization_barrier(jnp.concatenate([points * inverse_scale[:, None], targets], axis=0))
+    known = jnp.concatenate([points * inverse_scale[:, None], targets], axis=0)
+    known, noise_terms = lax.optimization_barrier((known, noise * targets))
     targets = known[NFEAT:]
     left = gather(known, "row", rows)
     right = lax.all_gather(known[:NFEAT], "col", axis=0)
 
     partial = image_terms(first_kernel, NRHS, left, right)
-    image = jnp.sum(exchange(partial, "col"), axis=0) + noise * targets
+    image = jnp.sum(exchange(partial, "col"), axis=0) + noise_terms
     partial = image_terms(second_kernel, NRHS + SUMS, left, right, gather(image, "row", rows))
     reduced = jnp.sum(exchange(partial, "col"), axis=0)
     image_image = reduced[:NRHS] + noise * image
@@ -165,12 +166,12 @@
     step_size = (norm_now / curvature)[:, None]
     residual = targets - step_size * image
     residual_image = image - step_size * image_image
-    sums = tile_of([inner(residual, residual), inner(residual, residual_image), inner(residual, image)])
+    sums = row_of([inner(residual, residual), inner(residual, residual_image), inner(residual, image)])
     sums = jnp.sum(gather(sums, "col", cols), axis=0)
-    sums = jnp.sum(gather(sums, "row", rows), axis=0)
-    norm_next = sums[0, :NRHS]
+    sums = jnp.sum(gather(sums, "row", rows), axis=0)[0]
+    norm_next = sums[:NRHS]
     ratio = norm_next / norm_now
-    next_curvature = sums[1, :NRHS] + ratio * (2.0 * sums[2, :NRHS] + ratio * curvature)
+    next_curvature = sums[NRHS : 2 * NRHS] + ratio * (2.0 * sums[2 * NRHS : 3 * NRHS] + ratio * curvature)
     next_step = (norm_next / next_curvature)[:, None]
     ratio = ratio[:, None]
     solution = step_size * targets + next_step * (residual + ratio * targets)

time: 130 us -> 127 us (0.977)
  blocking collectives: 95.6 us -> 93.6 us
    all_to_all x5, blocking collectives: 71.5 us -> 69.4 us  [exchange(): return lax.all_to_all(blocks, axis, 0, 0, tiled=True)]
where the time goes in v6:
time: 127 us
  blocking collectives  93.6 us (74%)
  Pallas kernels  18.4 us (14%)
  starting transfers between devices  10.5 us (8%)
  other arithmetic  2.06 us (2%)
  local copies, waits for them, and re-layouts  1.46 us (1%)
    all_to_all x5, blocking collectives, exchange(): return lax.all_to_all(blocks, axis, 0, 0, tiled=True)  69.4 us
    all_gather x1, blocking collectives, on_device(): right = lax.all_gather(known[:NFEAT], 'col', axis=0)  24.1 us
    pallas_call x2, Pallas kernels, image_terms(): pl.pallas_call(body, out_shape=jax.ShapeDtypeStruct((right.shape[0], rows...  18.4 us
    all_to_all x1, starting transfers between devices, exchange(): return lax.all_to_all(blocks, axis, 0, 0, tiled=True)  10.5 us
  transfers between devices with their start and end apart: 1, of which 0 were waited for; matrix products, arithmetic and copies ran while one was open for 0% of the time, Pallas kernels for 0%

profile of v6, /device:TPU:1, one launch (start us, length us, event | category | flops | bytes accessed | tf_op | source)
XLA Modules:
  0.0 126.7 jit_solution(13686137224672115200)
XLA Ops:
  0.6 0.0 copy-start
  0.6 0.8 broadcast_multiply_fusion.1
  1.4 0.0 copy-done
  1.4 0.0 copy-start.1
  1.4 0.6 copy-done.1
  2.1 0.1 broadcast_multiply_fusion
  2.1 0.8 broadcast_in_dim.8
  2.9 10.5 %all-to-all-start = ((f32[32,24,128]{2,1,0:T(8,128)}), f32[32,24,128]{2,1,0:T(8,128)S(1)}, u32[]{:S(2)}, u32[]{:S(2)}) async-start(f32[32,24,128]{2,1,0:T(8,128)} %broadcast_in_dim.8), calls=%async_computation | async-start | bytes 786432 | tf_op jit(solution)/shard_map/all_to_all | solution.py:136
  13.4 24.1 %all-gather = f32[128,128]{1,0:T(8,128)S(1)} all-gather(f32[8,128]{1,0:T(8,128)S(1)} %slice.31), channel_id=2, replica_groups=mesh['row'=32,'col'=16] {'col'}, dimensions={0}, use_global_device_ids=true | all-gather | bytes 69632 | tf_op jit(solution)/shard_map/all_gather | solution.py:157
  37.5 0.0 all-to-all-done.left_ref
  37.5 9.2 %shard_map.59 = f32[16,16,128]{2,1,0:T(8,128)S(1)} custom-call(f32[32,24,128]{2,1,0:T(8,128)S(1)} %all-to-all-done.left_ref, f32[16,8,128]{2,1,0:T(8,128)S(1)} %bitcast.31), custom_call_target="tpu_custom_call" | custom-call | tf_op jit(solution)/shard_map/pallas_call | solution.py:120
  46.7 11.9 %all_to_all.30 = f32[16,16,128]{2,1,0:T(8,128)S(1)} all-to-all(f32[16,16,128]{2,1,0:T(8,128)S(1)} %shard_map.59), channel_id=1, replica_groups=mesh['row'=32,'col'=16] {'col'}, dimensions={0} | all-to-all | bytes 262144 | tf_op jit(solution)/shard_map/all_to_all | solution.py:136
  58.7 21.6 %all_to_all.31.image_ref = f32[32,16,128]{2,1,0:T(8,128)S(1)} all-to-all(f32[32,16,128]{2,1,0:T(8,128)S(1)} %broadcast_in_dim.9), channel_id=1, replica_groups=mesh['row'=32,'col'=16] {'row'}, dimensions={0} | all-to-all | bytes 524288 | tf_op jit(solution)/shard_map/all_to_all | solution.py:136
  80.3 9.2 %shard_map.60 = f32[16,24,128]{2,1,0:T(8,128)S(1)} custom-call(f32[32,24,128]{2,1,0:T(8,128)S(1)} %all-to-all-done.left_ref, f32[16,8,128]{2,1,0:T(8,128)S(1)} %bitcast.32, f32[32,16,128]{2,1,0:T(8,128)S(1)} %all_to_all.31.image_ref), custom_call_target="tpu_custom_call" | custom-call | tf_op jit(solution)/shard_map/pallas_call | solution.py:120
  89.5 14.3 %all_to_all.32 = f32[16,24,128]{2,1,0:T(8,128)S(1)} all-to-all(f32[16,24,128]{2,1,0:T(8,128)S(1)} %shard_map.60), channel_id=1, replica_groups=mesh['row'=32,'col'=16] {'col'}, dimensions={0} | all-to-all | bytes 393216 | tf_op jit(solution)/shard_map/all_to_all | solution.py:136
  103.8 0.1 fusion.5
  103.9 0.2 multiply_reduce_fusion.2
  104.1 0.1 select_maximum_fusion
  104.2 9.7 %all_to_all.33 = f32[16,1,128]{2,1,0:T(1,128)S(1)} all-to-all(f32[16,1,128]{2,1,0:T(1,128)S(1)} %broadcast_in_dim.10), channel_id=1, replica_groups=mesh['row'=32,'col'=16] {'col'}, dimensions={0} | all-to-all | bytes 16384 | tf_op jit(solution)/shard_map/all_to_all | solution.py:136
  113.9 12.0 %all_to_all.34 = f32[32,1,128]{2,1,0:T(1,128)S(1)} all-to-all(f32[32,1,128]{2,1,0:T(1,128)S(1)} %broadcast_in_dim.11), channel_id=1, replica_groups=mesh['row'=32,'col'=16] {'row'}, dimensions={0} | all-to-all | bytes 32768 | tf_op jit(solution)/shard_map/all_to_all | solution.py:136
  125.9 0.1 fusion.4
  126.0 0.7 multiply_subtract_fusion
  (10 shorter events, 0.1 us)
Async XLA Ops:
  0.6 0.8 copy-start
  1.4 0.7 copy-start.1
  2.9 34.6 %all-to-all-start = ((f32[32,24,128]{2,1,0:T(8,128)}), f32[32,24,128]{2,1,0:T(8,128)S(1)}, u32[]{:S(2)}, u32[]{:S(2)}) async-start(f32[32,24,128]{2,1,0:T(8,128)} %broadcast_in_dim.8), calls=%async_computation | async-start | bytes 786432 | tf_op jit(solution)/shard_map/all_to_all | solution.py:136

commit v7 on v6

--- a/solution.py
+++ b/solution.py
@@ -8,6 +8,10 @@
 from jax.experimental.pallas import tpu as pltpu
 from jax.sharding import PartitionSpec as P
 
+AXES = ("y", "x", "z", "core")
+SHAPE = (8, 4, 8, 2)
+ROW = ("x", "z")
+COL = ("y", "core")
 LANES = 128
 NFEAT = 8
 NRHS = 16
@@ -151,15 +155,16 @@
 def on_device(rows, cols, points, inverse_scale, targets, noise_var):
     noise = noise_var[:, None]
     known = jnp.concatenate([points * inverse_scale[:, None], targets], axis=0)
-    known, noise_terms = lax.optimization_barrier((known, noise * targets))
+    known = lax.optimization_barrier(known)
     targets = known[NFEAT:]
-    left = gather(known, "row", rows)
-    right = lax.all_gather(known[:NFEAT], "col", axis=0)
+    left = gather(known, ROW, rows)
+    right = lax.all_gather(known[:NFEAT], COL, axis=0)
+    right, noise_terms = lax.optimization_barrier((right, noise * targets))
 
     partial = image_terms(first_kernel, NRHS, left, right)
-    image = jnp.sum(exchange(partial, "col"), axis=0) + noise_terms
-    partial = image_terms(second_kernel, NRHS + SUMS, left, right, gather(image, "row", rows))
-    reduced = jnp.sum(exchange(partial, "col"), axis=0)
+    image = jnp.sum(exchange(partial, COL), axis=0) + noise_terms
+    partial = image_terms(second_kernel, NRHS + SUMS, left, right, gather(image, ROW, rows))
+    reduced = jnp.sum(exchange(partial, COL), axis=0)
     image_image = reduced[:NRHS] + noise * image
 
     norm_now, curvature = reduced[NRHS, :NRHS], reduced[NRHS, NRHS : 2 * NRHS]
@@ -167,8 +172,8 @@
     residual = targets - step_size * image
     residual_image = image - step_size * image_image
     sums = row_of([inner(residual, residual), inner(residual, residual_image), inner(residual, image)])
-    sums = jnp.sum(gather(sums, "col", cols), axis=0)
-    sums = jnp.sum(gather(sums, "row", rows), axis=0)[0]
+    sums = jnp.sum(gather(sums, COL, cols), axis=0)
+    sums = jnp.sum(gather(sums, ROW, rows), axis=0)[0]
     norm_next = sums[:NRHS]
     ratio = norm_next / norm_now
     next_curvature = sums[NRHS : 2 * NRHS] + ratio * (2.0 * sums[2 * NRHS : 3 * NRHS] + ratio * curvature)
@@ -179,11 +184,16 @@
     return (solution, residual)
 
 
+def size_of(mesh, axes):
+    return math.prod(mesh.shape[axis] for axis in axes)
+
+
 def solution(mesh):
+    mesh = jax.sharding.Mesh(mesh.devices.reshape(SHAPE), AXES)
     return jax.shard_map(
-        functools.partial(on_device, mesh.shape["row"], mesh.shape["col"]),
+        functools.partial(on_device, size_of(mesh, ROW), size_of(mesh, COL)),
         mesh=mesh,
-        in_specs=(P(None, ("row", "col")), P(), P(None, ("row", "col")), P()),
-        out_specs=(P(None, ("row", "col")), P(None, ("row", "col"))),
+        in_specs=(P(None, AXES), P(), P(None, AXES), P()),
+        out_specs=(P(None, AXES), P(None, AXES)),
         check_vma=False,
     )

time: 127 us -> 126 us (level)
  blocking collectives: 93.6 us -> 89.7 us
  starting transfers between devices: 10.5 us -> 13.7 us
    all_gather x1, blocking collectives: 24.1 us -> 18.5 us  [on_device(): right = lax.all_gather(known[:NFEAT], COL, axis=0)]
    all_to_all x1, starting transfers between devices: 10.5 us -> 13.7 us  [exchange(): return lax.all_to_all(blocks, axis, 0, 0, tiled=True)]
    all_to_all x5, blocking collectives: 69.4 us -> 71.2 us  [exchange(): return lax.all_to_all(blocks, axis, 0, 0, tiled=True)]
where the time goes in v7:
time: 126 us; the launch traced here: 125 us
  blocking collectives  89.7 us (71%)
  Pallas kernels  18.4 us (15%)
  starting transfers between devices  13.7 us (11%)
  other arithmetic  2.06 us (2%)
    all_to_all x5, blocking collectives, exchange(): return lax.all_to_all(blocks, axis, 0, 0, tiled=True)  71.2 us
    all_gather x1, blocking collectives, on_device(): right = lax.all_gather(known[:NFEAT], COL, axis=0)  18.5 us
    pallas_call x2, Pallas kernels, image_terms(): pl.pallas_call(body, out_shape=jax.ShapeDtypeStruct((right.shape[0], rows...  18.4 us
    all_to_all x1, starting transfers between devices, exchange(): return lax.all_to_all(blocks, axis, 0, 0, tiled=True)  13.7 us
  transfers between devices with their start and end apart: 1, of which 0 were waited for; matrix products, arithmetic and copies ran while one was open for 0% of the time, Pallas kernels for 0%

profile of v7, /device:TPU:1, one launch (start us, length us, event | category | flops | bytes accessed | tf_op | source)
XLA Modules:
  0.0 125.4 jit_solution(15727329487319564401)
XLA Ops:
  0.6 0.0 copy-start
  0.6 0.8 broadcast_multiply_fusion
  1.4 0.0 copy-done
  1.4 0.8 broadcast_in_dim.8
  2.2 13.7 %all-to-all-start = ((f32[32,24,128]{2,1,0:T(8,128)}), f32[32,24,128]{2,1,0:T(8,128)S(1)}, u32[]{:S(2)}, u32[]{:S(2)}) async-start(f32[32,24,128]{2,1,0:T(8,128)} %broadcast_in_dim.8), calls=%async_computation | async-start | bytes 786432 | tf_op jit(solution)/shard_map/all_to_all | solution.py:140
  15.9 0.0 copy-start.1
  15.9 18.5 %all-gather = f32[128,128]{1,0:T(8,128)S(1)} all-gather(f32[8,128]{1,0:T(8,128)S(1)} %slice.41), channel_id=2, replica_groups=mesh['y'=8,'x'=4,'z'=8,'core'=2] {'y','core'}, dimensions={0}, use_global_device_ids=true | all-gather | bytes 69632 | tf_op jit(solution)/shard_map/all_gather | solution.py:161
  34.5 0.0 copy-done.1
  34.5 0.1 slice_multiply_fusion
  34.5 0.0 all-to-all-done.left_ref
  34.5 9.2 %shard_map.59 = f32[16,16,128]{2,1,0:T(8,128)S(1)} custom-call(f32[32,24,128]{2,1,0:T(8,128)S(1)} %all-to-all-done.left_ref, f32[16,8,128]{2,1,0:T(8,128)S(1)} %bitcast.31), custom_call_target="tpu_custom_call" | custom-call | tf_op jit(solution)/shard_map/pallas_call | solution.py:124
  43.8 13.5 %all_to_all.30 = f32[16,16,128]{2,1,0:T(8,128)S(1)} all-to-all(f32[16,16,128]{2,1,0:T(8,128)S(1)} %shard_map.59), channel_id=1, replica_groups=mesh['y'=8,'x'=4,'z'=8,'core'=2] {'y','core'}, dimensions={0} | all-to-all | bytes 262144 | tf_op jit(solution)/shard_map/all_to_all | solution.py:140
  57.3 20.0 %all_to_all.31.image_ref = f32[32,16,128]{2,1,0:T(8,128)S(1)} all-to-all(f32[32,16,128]{2,1,0:T(8,128)S(1)} %broadcast_in_dim.9), channel_id=1, replica_groups=mesh['y'=8,'x'=4,'z'=8,'core'=2] {'x','z'}, dimensions={0} | all-to-all | bytes 524288 | tf_op jit(solution)/shard_map/all_to_all | solution.py:140
  77.3 9.2 %shard_map.60 = f32[16,24,128]{2,1,0:T(8,128)S(1)} custom-call(f32[32,24,128]{2,1,0:T(8,128)S(1)} %all-to-all-done.left_ref, f32[16,8,128]{2,1,0:T(8,128)S(1)} %bitcast.32, f32[32,16,128]{2,1,0:T(8,128)S(1)} %all_to_all.31.image_ref), custom_call_target="tpu_custom_call" | custom-call | tf_op jit(solution)/shard_map/pallas_call | solution.py:124
  86.5 15.0 %all_to_all.32 = f32[16,24,128]{2,1,0:T(8,128)S(1)} all-to-all(f32[16,24,128]{2,1,0:T(8,128)S(1)} %shard_map.60), channel_id=1, replica_groups=mesh['y'=8,'x'=4,'z'=8,'core'=2] {'y','core'}, dimensions={0} | all-to-all | bytes 393216 | tf_op jit(solution)/shard_map/all_to_all | solution.py:140
  101.5 0.1 fusion.5
  101.6 0.2 multiply_reduce_fusion.2
  101.8 0.1 select_maximum_fusion
  101.9 9.7 %all_to_all.33 = f32[16,1,128]{2,1,0:T(1,128)S(1)} all-to-all(f32[16,1,128]{2,1,0:T(1,128)S(1)} %broadcast_in_dim.10), channel_id=1, replica_groups=mesh['y'=8,'x'=4,'z'=8,'core'=2] {'y','core'}, dimensions={0} | all-to-all | bytes 16384 | tf_op jit(solution)/shard_map/all_to_all | solution.py:140
  111.6 13.0 %all_to_all.34 = f32[32,1,128]{2,1,0:T(1,128)S(1)} all-to-all(f32[32,1,128]{2,1,0:T(1,128)S(1)} %broadcast_in_dim.11), channel_id=1, replica_groups=mesh['y'=8,'x'=4,'z'=8,'core'=2] {'x','z'}, dimensions={0} | all-to-all | bytes 32768 | tf_op jit(solution)/shard_map/all_to_all | solution.py:140
  124.7 0.1 fusion.4
  124.8 0.7 multiply_subtract_fusion
  (10 shorter events, 0.1 us)
Async XLA Ops:
  0.6 0.8 copy-start
  2.2 32.4 %all-to-all-start = ((f32[32,24,128]{2,1,0:T(8,128)}), f32[32,24,128]{2,1,0:T(8,128)S(1)}, u32[]{:S(2)}, u32[]{:S(2)}) async-start(f32[32,24,128]{2,1,0:T(8,128)} %broadcast_in_dim.8), calls=%async_computation | async-start | bytes 786432 | tf_op jit(solution)/shard_map/all_to_all | solution.py:140
  15.9 18.6 %copy-start.1 = (f32[16]{0:T(128)S(1)}, f32[16]{0:T(128)}, u32[]{:S(2)}) copy-start(f32[16]{0:T(128)} %param.7) | copy-start | bytes 196

commit v8 on v7

--- a/solution.py
+++ b/solution.py
@@ -86,9 +86,7 @@
     return jnp.concatenate([dot(vector[:, rows], high), dot(vector[:NRHS, rows], low)], axis=0)
 
 
-def multiply(left_ref, right_ref, value_of, out_ref, left, right, vector, total):
-    write_right(right_ref, right)
-    write_left(left_ref, left)
+def multiply(value_of, out_ref, left, right, vector, total):
     split_vector(value_of, vector)
     for place in range(total.shape[1] // WIDE):
         span = pl.ds(place * WIDE, WIDE)
@@ -97,12 +95,14 @@
     write_terms(total, out_ref)
 
 
-def first_kernel(left_ref, right_ref, out_ref, *scratch_refs):
-    multiply(left_ref, right_ref, lambda block: left_ref[block, NFEAT:, :], out_ref, *scratch_refs)
-
-
-def second_kernel(left_ref, right_ref, image_ref, out_ref, *scratch_refs):
-    multiply(left_ref, right_ref, lambda block: image_ref[block], out_ref, *scratch_refs)
+def first_kernel(left_ref, right_ref, out_ref, left, right, vector, total):
+    write_right(right_ref, right)
+    write_left(left_ref, left)
+    multiply(lambda block: left_ref[block, NFEAT:, :], out_ref, left, right, vector, total)
+
+
+def second_kernel(left_ref, image_ref, left, right, out_ref, vector, total):
+    multiply(lambda block: image_ref[block], out_ref, left, right, vector, total)
     square = jnp.zeros((NRHS, LANES), jnp.float32)
     product = jnp.zeros((NRHS, LANES), jnp.float32)
     for block in range(left_ref.shape[0]):
@@ -119,21 +119,39 @@
 VMEM_BLOCK = pl.BlockSpec(memory_space=pltpu.VMEM)
 
 
-def image_terms(body, rows, left, right, *others):
+def product_scratch(left_count, right_count):
+    return [
+        pltpu.VMEM((2 * NRHS, left_count), jnp.bfloat16),
+        pltpu.VMEM((3 * NRHS, right_count), jnp.float32),
+    ]
+
+
+def first_terms(left, right):
     left_count, right_count = left.shape[0] * LANES, right.shape[0] * LANES
     return pl.pallas_call(
-        body,
-        out_shape=jax.ShapeDtypeStruct((right.shape[0], rows, LANES), jnp.float32),
-        in_specs=[VMEM_BLOCK] * (2 + len(others)),
+        first_kernel,
+        out_shape=[
+            jax.ShapeDtypeStruct((right.shape[0], NRHS, LANES), jnp.float32),
+            jax.ShapeDtypeStruct((left_count, FEATURE_ROWS), jnp.bfloat16),
+            jax.ShapeDtypeStruct((FEATURE_ROWS, right_count), jnp.bfloat16),
+        ],
+        in_specs=[VMEM_BLOCK] * 2,
+        out_specs=[VMEM_BLOCK] * 3,
+        scratch_shapes=product_scratch(left_count, right_count),
+        compiler_params=pltpu.CompilerParams(vmem_limit_bytes=VMEM_LIMIT),
+    )(left, right)
+
+
+def second_terms(left, image, left_features, right_features):
+    left_count, right_count = left_features.shape[0], right_features.shape[1]
+    return pl.pallas_call(
+        second_kernel,
+        out_shape=jax.ShapeDtypeStruct((right_count // LANES, NRHS + SUMS, LANES), jnp.float32),
+        in_specs=[VMEM_BLOCK] * 4,
         out_specs=VMEM_BLOCK,
-        scratch_shapes=[
-            pltpu.VMEM((left_count, FEATURE_ROWS), jnp.bfloat16),
-            pltpu.VMEM((FEATURE_ROWS, right_count), jnp.bfloat16),
-            pltpu.VMEM((2 * NRHS, left_count), jnp.bfloat16),
-            pltpu.VMEM((3 * NRHS, right_count), jnp.float32),
-        ],
+        scratch_shapes=product_scratch(left_count, right_count),
         compiler_params=pltpu.CompilerParams(vmem_limit_bytes=VMEM_LIMIT),
-    )(left, right, *others)
+    )(left, image, left_features, right_features)
 
 
 def exchange(blocks, axis):
@@ -161,9 +179,9 @@
     right = lax.all_gather(known[:NFEAT], COL, axis=0)
     right, noise_terms = lax.optimization_barrier((right, noise * targets))
 
-    partial = image_terms(first_kernel, NRHS, left, right)
+    partial, *kept = first_terms(left, right)
     image = jnp.sum(exchange(partial, COL), axis=0) + noise_terms
-    partial = image_terms(second_kernel, NRHS + SUMS, left, right, gather(image, ROW, rows))
+    partial = second_terms(left, gather(image, ROW, rows), *kept)
     reduced = jnp.sum(exchange(partial, COL), axis=0)
     image_image = reduced[:NRHS] + noise * image
 

time: 126 us -> 126 us (level)
  no operation moved by 1% of the time
where the time goes in v8:
time: 126 us; the launch traced here: 125 us
  blocking collectives  89.7 us (71%)
  Pallas kernels  18.3 us (15%)
  starting transfers between devices  13.7 us (11%)
  other arithmetic  2.06 us (2%)
    all_to_all x5, blocking collectives, exchange(): return lax.all_to_all(blocks, axis, 0, 0, tiled=True)  71.2 us
    all_gather x1, blocking collectives, on_device(): right = lax.all_gather(known[:NFEAT], COL, axis=0)  18.5 us
    all_to_all x1, starting transfers between devices, exchange(): return lax.all_to_all(blocks, axis, 0, 0, tiled=True)  13.7 us
    pallas_call x1, Pallas kernels, first_terms(): pl.pallas_call(first_kernel, out_shape=[jax.ShapeDtypeStruct((right.shape...  9.21 us
    pallas_call x1, Pallas kernels, second_terms(): pl.pallas_call(second_kernel, out_shape=jax.ShapeDtypeStruct((right_count...  9.05 us
  transfers between devices with their start and end apart: 1, of which 0 were waited for; matrix products, arithmetic and copies ran while one was open for 0% of the time, Pallas kernels for 0%

profile of v8, /device:TPU:1, one launch (start us, length us, event | category | flops | bytes accessed | tf_op | source)
XLA Modules:
  0.0 125.3 jit_solution(2591671735377174452)
XLA Ops:
  0.6 0.0 copy-start
  0.6 0.8 broadcast_multiply_fusion
  1.4 0.0 copy-done
  1.4 0.8 broadcast_in_dim.8
  2.2 13.7 %all-to-all-start = ((f32[32,24,128]{2,1,0:T(8,128)}), f32[32,24,128]{2,1,0:T(8,128)S(1)}, u32[]{:S(2)}, u32[]{:S(2)}) async-start(f32[32,24,128]{2,1,0:T(8,128)} %broadcast_in_dim.8), calls=%async_computation | async-start | bytes 786432 | tf_op jit(solution)/shard_map/all_to_all | solution.py:158
  15.9 0.0 copy-start.1
  15.9 18.5 %all-gather = f32[128,128]{1,0:T(8,128)S(1)} all-gather(f32[8,128]{1,0:T(8,128)S(1)} %slice.41), channel_id=2, replica_groups=mesh['y'=8,'x'=4,'z'=8,'core'=2] {'y','core'}, dimensions={0}, use_global_device_ids=true | all-gather | bytes 69632 | tf_op jit(solution)/shard_map/all_gather | solution.py:179
  34.5 0.0 copy-done.1
  34.5 0.1 slice_multiply_fusion
  34.5 0.0 all-to-all-done.left_ref
  34.5 9.2 %shard_map.59 = (f32[16,16,128]{2,1,0:T(8,128)S(1)}, bf16[4096,64]{1,0:T(8,128)(2,1)S(1)}, bf16[64,2048]{1,0:T(8,128)(2,1)S(1)}) custom-call(f32[32,24,128]{2,1,0:T(8,128)S(1)} %all-to-all-done.left_ref, f32[16,8,128]{2,1,0:T(8,128)S(1)} %bitcast.31), custom_call_target="tpu_custom_call" | custom-call | tf_op jit(solution)/shard_map/pallas_call | solution.py:131
  43.8 13.5 %all_to_all.30 = f32[16,16,128]{2,1,0:T(8,128)S(1)} all-to-all(f32[16,16,128]{2,1,0:T(8,128)S(1)} %get-tuple-element.8), channel_id=1, replica_groups=mesh['y'=8,'x'=4,'z'=8,'core'=2] {'y','core'}, dimensions={0} | all-to-all | bytes 262144 | tf_op jit(solution)/shard_map/all_to_all | solution.py:158
  57.3 20.0 %all_to_all.31.image_ref = f32[32,16,128]{2,1,0:T(8,128)S(1)} all-to-all(f32[32,16,128]{2,1,0:T(8,128)S(1)} %broadcast_in_dim.9), channel_id=1, replica_groups=mesh['y'=8,'x'=4,'z'=8,'core'=2] {'x','z'}, dimensions={0} | all-to-all | bytes 524288 | tf_op jit(solution)/shard_map/all_to_all | solution.py:158
  77.3 9.1 %shard_map.60 = f32[16,24,128]{2,1,0:T(8,128)S(1)} custom-call(f32[32,24,128]{2,1,0:T(8,128)S(1)} %all-to-all-done.left_ref, f32[32,16,128]{2,1,0:T(8,128)S(1)} %all_to_all.31.image_ref, bf16[4096,64]{1,0:T(8,128)(2,1)S(1)} %get-tuple-element.10.left, bf16[64,2048]{1,0:T(8,128)(2,1)S(1)} %get-tuple-element.11.right), custom_call_target="tpu_custom_call" | custom-call | tf_op jit(solution)/shard_map/pallas_call | solution.py:147
  86.3 15.0 %all_to_all.32 = f32[16,24,128]{2,1,0:T(8,128)S(1)} all-to-all(f32[16,24,128]{2,1,0:T(8,128)S(1)} %shard_map.60), channel_id=1, replica_groups=mesh['y'=8,'x'=4,'z'=8,'core'=2] {'y','core'}, dimensions={0} | all-to-all | bytes 393216 | tf_op jit(solution)/shard_map/all_to_all | solution.py:158
  101.4 0.1 fusion.5
  101.4 0.2 multiply_reduce_fusion.2
  101.7 0.1 select_maximum_fusion
  101.8 9.7 %all_to_all.33 = f32[16,1,128]{2,1,0:T(1,128)S(1)} all-to-all(f32[16,1,128]{2,1,0:T(1,128)S(1)} %broadcast_in_dim.10), channel_id=1, replica_groups=mesh['y'=8,'x'=4,'z'=8,'core'=2] {'y','core'}, dimensions={0} | all-to-all | bytes 16384 | tf_op jit(solution)/shard_map/all_to_all | solution.py:158
  111.5 13.0 %all_to_all.34 = f32[32,1,128]{2,1,0:T(1,128)S(1)} all-to-all(f32[32,1,128]{2,1,0:T(1,128)S(1)} %broadcast_in_dim.11), channel_id=1, replica_groups=mesh['y'=8,'x'=4,'z'=8,'core'=2] {'x','z'}, dimensions={0} | all-to-all | bytes 32768 | tf_op jit(solution)/shard_map/all_to_all | solution.py:158
  124.5 0.1 fusion.4
  124.6 0.7 multiply_subtract_fusion
  (10 shorter events, 0.1 us)
Async XLA Ops:
  0.6 0.8 copy-start
  2.2 32.4 %all-to-all-start = ((f32[32,24,128]{2,1,0:T(8,128)}), f32[32,24,128]{2,1,0:T(8,128)S(1)}, u32[]{:S(2)}, u32[]{:S(2)}) async-start(f32[32,24,128]{2,1,0:T(8,128)} %broadcast_in_dim.8), calls=%async_computation | async-start | bytes 786432 | tf_op jit(solution)/shard_map/all_to_all | solution.py:158
  15.9 18.6 %copy-start.1 = (f32[16]{0:T(128)S(1)}, f32[16]{0:T(128)}, u32[]{:S(2)}) copy-start(f32[16]{0:T(128)} %param.7) | copy-start | bytes 196

commit v9 on v7

--- a/solution.py
+++ b/solution.py
@@ -154,11 +154,10 @@
 
 def on_device(rows, cols, points, inverse_scale, targets, noise_var):
     noise = noise_var[:, None]
-    known = jnp.concatenate([points * inverse_scale[:, None], targets], axis=0)
-    known = lax.optimization_barrier(known)
-    targets = known[NFEAT:]
-    left = gather(known, ROW, rows)
-    right = lax.all_gather(known[:NFEAT], COL, axis=0)
+    scaled = points * inverse_scale[:, None]
+    spread = [jnp.broadcast_to(block[None], (rows,) + block.shape) for block in (scaled, targets)]
+    left = exchange(jnp.concatenate(spread, axis=1), ROW)
+    right = lax.all_gather(scaled, COL, axis=0)
     right, noise_terms = lax.optimization_barrier((right, noise * targets))
 
     partial = image_terms(first_kernel, NRHS, left, right)

time: 126 us -> 127 us (level)
  no operation moved by 1% of the time
where the time goes in v9:
time: 127 us; the launch traced here: 126 us
  blocking collectives  89.7 us (71%)
  Pallas kernels  18.4 us (14%)
  starting transfers between devices  13.7 us (11%)
  other arithmetic  2.82 us (2%)
    all_to_all x5, blocking collectives, exchange(): return lax.all_to_all(blocks, axis, 0, 0, tiled=True)  71.2 us
    all_gather x1, blocking collectives, on_device(): right = lax.all_gather(scaled, COL, axis=0)  18.5 us
    pallas_call x2, Pallas kernels, image_terms(): pl.pallas_call(body, out_shape=jax.ShapeDtypeStruct((right.shape[0], rows...  18.4 us
    all_to_all x1, starting transfers between devices, exchange(): return lax.all_to_all(blocks, axis, 0, 0, tiled=True)  13.7 us
  transfers between devices with their start and end apart: 1, of which 0 were waited for; matrix products, arithmetic and copies ran while one was open for 0% of the time, Pallas kernels for 0%

profile of v9, /device:TPU:1, one launch (start us, length us, event | category | flops | bytes accessed | tf_op | source)
XLA Modules:
  0.0 126.1 jit_solution(13734150515209158054)
XLA Ops:
  0.6 0.8 broadcast_multiply_fusion.1
  1.4 0.0 copy-start
  1.4 0.7 copy-done
  2.1 0.8 pad_maximum_fusion
  2.9 13.7 %all-to-all-start = ((f32[32,24,128]{2,1,0:T(8,128)}), f32[32,24,128]{2,1,0:T(8,128)S(1)}, u32[]{:S(2)}, u32[]{:S(2)}) async-start(f32[32,24,128]{2,1,0:T(8,128)} %pad_maximum_fusion), calls=%async_computation | async-start | bytes 786432 | tf_op jit(solution)/shard_map/all_to_all | solution.py:140
  16.6 0.0 copy-start.1
  16.6 18.5 %all-gather = f32[128,128]{1,0:T(8,128)S(1)} all-gather(f32[8,128]{1,0:T(8,128)S(1)} %broadcast_multiply_fusion.1), channel_id=2, replica_groups=mesh['y'=8,'x'=4,'z'=8,'core'=2] {'y','core'}, dimensions={0}, use_global_device_ids=true | all-gather | bytes 69632 | tf_op jit(solution)/shard_map/all_gather | solution.py:160
  35.2 0.0 copy-done.1
  35.2 0.1 broadcast_multiply_fusion
  35.2 0.0 all-to-all-done.left_ref
  35.2 9.2 %shard_map.59 = f32[16,16,128]{2,1,0:T(8,128)S(1)} custom-call(f32[32,24,128]{2,1,0:T(8,128)S(1)} %all-to-all-done.left_ref, f32[16,8,128]{2,1,0:T(8,128)S(1)} %bitcast.31), custom_call_target="tpu_custom_call" | custom-call | tf_op jit(solution)/shard_map/pallas_call | solution.py:124
  44.4 13.5 %all_to_all.30 = f32[16,16,128]{2,1,0:T(8,128)S(1)} all-to-all(f32[16,16,128]{2,1,0:T(8,128)S(1)} %shard_map.59), channel_id=1, replica_groups=mesh['y'=8,'x'=4,'z'=8,'core'=2] {'y','core'}, dimensions={0} | all-to-all | bytes 262144 | tf_op jit(solution)/shard_map/all_to_all | solution.py:140
  58.0 20.0 %all_to_all.31.image_ref = f32[32,16,128]{2,1,0:T(8,128)S(1)} all-to-all(f32[32,16,128]{2,1,0:T(8,128)S(1)} %broadcast_in_dim.15), channel_id=1, replica_groups=mesh['y'=8,'x'=4,'z'=8,'core'=2] {'x','z'}, dimensions={0} | all-to-all | bytes 524288 | tf_op jit(solution)/shard_map/all_to_all | solution.py:140
  78.0 9.2 %shard_map.60 = f32[16,24,128]{2,1,0:T(8,128)S(1)} custom-call(f32[32,24,128]{2,1,0:T(8,128)S(1)} %all-to-all-done.left_ref, f32[16,8,128]{2,1,0:T(8,128)S(1)} %bitcast.32, f32[32,16,128]{2,1,0:T(8,128)S(1)} %all_to_all.31.image_ref), custom_call_target="tpu_custom_call" | custom-call | tf_op jit(solution)/shard_map/pallas_call | solution.py:124
  87.2 15.0 %all_to_all.32 = f32[16,24,128]{2,1,0:T(8,128)S(1)} all-to-all(f32[16,24,128]{2,1,0:T(8,128)S(1)} %shard_map.60), channel_id=1, replica_groups=mesh['y'=8,'x'=4,'z'=8,'core'=2] {'y','core'}, dimensions={0} | all-to-all | bytes 393216 | tf_op jit(solution)/shard_map/all_to_all | solution.py:140
  102.2 0.1 fusion.5
  102.3 0.2 multiply_reduce_fusion.2
  102.5 0.1 select_maximum_fusion
  102.6 9.7 %all_to_all.33 = f32[16,1,128]{2,1,0:T(1,128)S(1)} all-to-all(f32[16,1,128]{2,1,0:T(1,128)S(1)} %broadcast_in_dim.16), channel_id=1, replica_groups=mesh['y'=8,'x'=4,'z'=8,'core'=2] {'y','core'}, dimensions={0} | all-to-all | bytes 16384 | tf_op jit(solution)/shard_map/all_to_all | solution.py:140
  112.3 13.0 %all_to_all.34 = f32[32,1,128]{2,1,0:T(1,128)S(1)} all-to-all(f32[32,1,128]{2,1,0:T(1,128)S(1)} %broadcast_in_dim.17), channel_id=1, replica_groups=mesh['y'=8,'x'=4,'z'=8,'core'=2] {'x','z'}, dimensions={0} | all-to-all | bytes 32768 | tf_op jit(solution)/shard_map/all_to_all | solution.py:140
  125.4 0.1 fusion.4
  125.4 0.7 multiply_subtract_fusion
  (10 shorter events, 0.2 us)
Async XLA Ops:
  1.4 0.7 copy-start
  2.9 32.4 %all-to-all-start = ((f32[32,24,128]{2,1,0:T(8,128)}), f32[32,24,128]{2,1,0:T(8,128)S(1)}, u32[]{:S(2)}, u32[]{:S(2)}) async-start(f32[32,24,128]{2,1,0:T(8,128)} %pad_maximum_fusion), calls=%async_computation | async-start | bytes 786432 | tf_op jit(solution)/shard_map/all_to_all | solution.py:140
  16.6 18.6 %copy-start.1 = (f32[16]{0:T(128)S(1)}, f32[16]{0:T(128)}, u32[]{:S(2)}) copy-start(f32[16]{0:T(128)} %param.7) | copy-start | bytes 196

commit v10 on v8

--- a/solution.py
+++ b/solution.py
@@ -10,7 +10,7 @@
 
 AXES = ("y", "x", "z", "core")
 SHAPE = (8, 4, 8, 2)
-ROW = ("x", "z")
+ROW = ("z", "x")
 COL = ("y", "core")
 LANES = 128
 NFEAT = 8

time: 126 us -> 126 us (level)
  no operation moved by 1% of the time
where the time goes in v10:
time: 126 us; the launch traced here: 125 us
  blocking collectives  89.6 us (71%)
  Pallas kernels  18.3 us (15%)
  starting transfers between devices  13.7 us (11%)
  other arithmetic  2.06 us (2%)
    all_to_all x5, blocking collectives, exchange(): return lax.all_to_all(blocks, axis, 0, 0, tiled=True)  71 us
    all_gather x1, blocking collectives, on_device(): right = lax.all_gather(known[:NFEAT], COL, axis=0)  18.5 us
    all_to_all x1, starting transfers between devices, exchange(): return lax.all_to_all(blocks, axis, 0, 0, tiled=True)  13.7 us
    pallas_call x1, Pallas kernels, first_terms(): pl.pallas_call(first_kernel, out_shape=[jax.ShapeDtypeStruct((right.shape...  9.21 us
    pallas_call x1, Pallas kernels, second_terms(): pl.pallas_call(second_kernel, out_shape=jax.ShapeDtypeStruct((right_count...  9.05 us
  transfers between devices with their start and end apart: 1, of which 0 were waited for; matrix products, arithmetic and copies ran while one was open for 0% of the time, Pallas kernels for 0%

profile of v10, /device:TPU:1, one launch (start us, length us, event | category | flops | bytes accessed | tf_op | source)
XLA Modules:
  0.0 125.1 jit_solution(8185598343193385117)
XLA Ops:
  0.6 0.0 copy-start
  0.6 0.8 broadcast_multiply_fusion
  1.4 0.0 copy-done
  1.4 0.8 broadcast_in_dim.8
  2.2 13.7 %all-to-all-start = ((f32[32,24,128]{2,1,0:T(8,128)}), f32[32,24,128]{2,1,0:T(8,128)S(1)}, u32[]{:S(2)}, u32[]{:S(2)}) async-start(f32[32,24,128]{2,1,0:T(8,128)} %broadcast_in_dim.8), calls=%async_computation | async-start | bytes 786432 | tf_op jit(solution)/shard_map/all_to_all | solution.py:158
  15.9 0.0 copy-start.1
  15.9 18.5 %all-gather = f32[128,128]{1,0:T(8,128)S(1)} all-gather(f32[8,128]{1,0:T(8,128)S(1)} %slice.41), channel_id=2, replica_groups=mesh['y'=8,'x'=4,'z'=8,'core'=2] {'y','core'}, dimensions={0}, use_global_device_ids=true | all-gather | bytes 69632 | tf_op jit(solution)/shard_map/all_gather | solution.py:179
  34.5 0.0 copy-done.1
  34.5 0.1 slice_multiply_fusion
  34.5 0.0 all-to-all-done.left_ref
  34.5 9.2 %shard_map.59 = (f32[16,16,128]{2,1,0:T(8,128)S(1)}, bf16[4096,64]{1,0:T(8,128)(2,1)S(1)}, bf16[64,2048]{1,0:T(8,128)(2,1)S(1)}) custom-call(f32[32,24,128]{2,1,0:T(8,128)S(1)} %all-to-all-done.left_ref, f32[16,8,128]{2,1,0:T(8,128)S(1)} %bitcast.31), custom_call_target="tpu_custom_call" | custom-call | tf_op jit(solution)/shard_map/pallas_call | solution.py:131
  43.8 13.7 %all_to_all.30 = f32[16,16,128]{2,1,0:T(8,128)S(1)} all-to-all(f32[16,16,128]{2,1,0:T(8,128)S(1)} %get-tuple-element.8), channel_id=1, replica_groups=mesh['y'=8,'x'=4,'z'=8,'core'=2] {'y','core'}, dimensions={0} | all-to-all | bytes 262144 | tf_op jit(solution)/shard_map/all_to_all | solution.py:158
  57.5 21.3 %all_to_all.31.image_ref = f32[32,16,128]{2,1,0:T(8,128)S(1)} all-to-all(f32[32,16,128]{2,1,0:T(8,128)S(1)} %broadcast_in_dim.9), channel_id=1, replica_groups=mesh['y'=8,'x'=4,'z'=8,'core'=2] {'z','x'}, dimensions={0} | all-to-all | bytes 524288 | tf_op jit(solution)/shard_map/all_to_all | solution.py:158
  78.9 9.1 %shard_map.60 = f32[16,24,128]{2,1,0:T(8,128)S(1)} custom-call(f32[32,24,128]{2,1,0:T(8,128)S(1)} %all-to-all-done.left_ref, f32[32,16,128]{2,1,0:T(8,128)S(1)} %all_to_all.31.image_ref, bf16[4096,64]{1,0:T(8,128)(2,1)S(1)} %get-tuple-element.10.left, bf16[64,2048]{1,0:T(8,128)(2,1)S(1)} %get-tuple-element.11.right), custom_call_target="tpu_custom_call" | custom-call | tf_op jit(solution)/shard_map/pallas_call | solution.py:147
  87.9 14.3 %all_to_all.32 = f32[16,24,128]{2,1,0:T(8,128)S(1)} all-to-all(f32[16,24,128]{2,1,0:T(8,128)S(1)} %shard_map.60), channel_id=1, replica_groups=mesh['y'=8,'x'=4,'z'=8,'core'=2] {'y','core'}, dimensions={0} | all-to-all | bytes 393216 | tf_op jit(solution)/shard_map/all_to_all | solution.py:158
  102.3 0.1 fusion.5
  102.4 0.2 multiply_reduce_fusion.2
  102.6 0.1 select_maximum_fusion
  102.7 9.7 %all_to_all.33 = f32[16,1,128]{2,1,0:T(1,128)S(1)} all-to-all(f32[16,1,128]{2,1,0:T(1,128)S(1)} %broadcast_in_dim.10), channel_id=1, replica_groups=mesh['y'=8,'x'=4,'z'=8,'core'=2] {'y','core'}, dimensions={0} | all-to-all | bytes 16384 | tf_op jit(solution)/shard_map/all_to_all | solution.py:158
  112.4 12.0 %all_to_all.34 = f32[32,1,128]{2,1,0:T(1,128)S(1)} all-to-all(f32[32,1,128]{2,1,0:T(1,128)S(1)} %broadcast_in_dim.11), channel_id=1, replica_groups=mesh['y'=8,'x'=4,'z'=8,'core'=2] {'z','x'}, dimensions={0} | all-to-all | bytes 32768 | tf_op jit(solution)/shard_map/all_to_all | solution.py:158
  124.4 0.1 fusion.4
  124.5 0.7 multiply_subtract_fusion
  (10 shorter events, 0.1 us)
Async XLA Ops:
  0.6 0.8 copy-start
  2.2 32.4 %all-to-all-start = ((f32[32,24,128]{2,1,0:T(8,128)}), f32[32,24,128]{2,1,0:T(8,128)S(1)}, u32[]{:S(2)}, u32[]{:S(2)}) async-start(f32[32,24,128]{2,1,0:T(8,128)} %broadcast_in_dim.8), calls=%async_computation | async-start | bytes 786432 | tf_op jit(solution)/shard_map/all_to_all | solution.py:158
  15.9 18.6 %copy-start.1 = (f32[16]{0:T(128)S(1)}, f32[16]{0:T(128)}, u32[]{:S(2)}) copy-start(f32[16]{0:T(128)} %param.7) | copy-start | bytes 196
